TPU v7x, 512 devices: a whole 4x4x16 slice. The times are simulated.
512 devices in a mesh: dp: 64 (over x, z), mp: 8 (over y, core).
Axes of the slice: x: 4, y: 4, z: 16, core: 2. Of those that a mesh axis runs over, the one named last changes fastest.
Arguments:
- features: bfloat16 [32768, 1536], P('dp'), may hold values from -36 to 36
- frame_start: int32 [64], P('dp'), may hold values from 0 to 384
- chan_start: int32 [64], P('dp'), may hold values from 0 to 1344
- master_weight: float32 [1536, 6144], P('dp', 'mp'), may hold values from -0.15625 to 0.15625
- row_moment: float32 [1536], P('dp'), may hold values from 0.1 to 3
- col_moment: float32 [6144], P('mp'), may hold values from 0.1 to 3
- out_grad: bfloat16 [32768, 6144], P('dp', 'mp'), may hold values from -36 to 36
Outputs:
- new_master: float32 [1536, 6144], P('dp', 'mp')
- row_state: float32 [1536], P('dp')
- col_state: float32 [6144], P('mp')
- compute_weight: bfloat16 [1536, 6144], P(None, 'mp')
All inputs are finite; a program needn't handle non-finite values.
Results may differ from a plain program's by a relative error of at most 0.0023.
The roundings to bfloat16 on the way count: a program that leaves them out, or rounds other values in their place, can miss the bound.
Values may be sent and summed in bfloat16 or wider, within the bound.
A program may use at most 64 MiB of HBM per device.

v0:
```python
import jax
import jax.numpy as jnp
from jax import lax
from jax.sharding import PartitionSpec as P

D = 1536
FF = 6144
TMASK = 128
FMASK = 192


epsilon = 1e-06
decay_rate = 0.8
step_rate = 0.01


def per_device(features, frame_start, chan_start, master_weight, row_moment, col_moment, out_grad):
    frame_count = features.shape[0]
    feature_count = features.shape[1]
    offset = lax.broadcasted_iota(jnp.int32, (frame_count, 1), 0)
    channel = lax.broadcasted_iota(jnp.int32, (1, feature_count), 1)
    first_frame = frame_start[0]
    first_chan = chan_start[0]
    time_keep = (offset < first_frame) | (offset >= first_frame + TMASK)
    chan_keep = (channel < first_chan) | (channel >= first_chan + FMASK)
    masked = jnp.where(time_keep & chan_keep, features, jnp.zeros_like(features))
    weight_low = master_weight.astype(jnp.bfloat16)
    weight_full = lax.all_gather(weight_low, "dp", axis=0, tiled=True)
    pre = jnp.dot(masked, weight_full, preferred_element_type=jnp.float32)
    sigmoid_pre = jax.nn.sigmoid(pre)
    slope = sigmoid_pre + pre * sigmoid_pre * (1.0 - sigmoid_pre)
    dpre = (out_grad.astype(jnp.float32) * slope).astype(jnp.bfloat16)
    grad = lax.psum_scatter(
        lax.dot_general(masked, dpre, (((0,), (0,)), ((), ())), preferred_element_type=jnp.float32),
        "dp",
        scatter_dimension=0,
        tiled=True,
    )
    squared = grad * grad
    row_local = jnp.sum(squared, axis=1)
    col_local = jnp.sum(squared, axis=0)
    norm_local = jnp.sum(row_local)
    col_total = lax.psum(col_local, "dp")
    row_total = lax.psum(row_local, "mp")
    total = lax.psum(norm_local, ("dp", "mp"))
    clip = 1.0 / jnp.maximum(1.0, jnp.sqrt(total / (D * FF)))
    row_state = decay_rate * row_moment + (1.0 - decay_rate) * (
        clip * clip * row_total / FF + epsilon
    )
    row_mean = lax.psum(jnp.sum(row_state), "dp") / D
    col_state = decay_rate * col_moment + (1.0 - decay_rate) * (
        clip * clip * col_total / D + epsilon
    )
    update = clip * grad * lax.rsqrt(row_state[:, None] * col_state[None, :] / row_mean)
    new_master = master_weight - step_rate * update
    compute_weight = lax.all_gather(new_master.astype(jnp.bfloat16), "dp", axis=0, tiled=True)
    return (new_master, row_state, col_state, compute_weight)


def solution(mesh):
    placed = (P("dp", None), P("dp"), P("dp"), P("dp", "mp"), P("dp"), P("mp"), P("dp", "mp"))
    return jax.shard_map(
        per_device,
        mesh=mesh,
        in_specs=placed,
        out_specs=(P("dp", "mp"), P("dp"), P("mp"), P(None, "mp")),
        check_vma=False,
    )
```

profile of v0, /device:TPU:24, one launch (start us, length us, event | category | flops | bytes accessed | tf_op | source)
XLA Modules:
  0.0 1264.7 jit_solution(2935742438948479913)
XLA Ops:
  7.2 0.0 all-gather.3.cloned.1.call-start
  7.2 1.5 convert_element_type.13
  8.7 0.0 all-gather.3.cloned.1.call-update
  8.7 0.0 reduce-scatter.2.cloned.1.call-start
  10.1 147.8 %all-gather.3.cloned.1.call-done = bf16[1536,768]{1,0:T(8,128)(2,1)} async-done(((bf16[24,768]{1,0:T(8,128)(2,1)}), bf16[1536,768]{1,0:T(8,128)(2,1)}) %all-gather.3.cloned.1.call-update) | async-done | bytes 2359312 | tf_op jit(solution)/shard_map/all_gather | solution.py:28
  157.9 8.0 fusion
  165.9 0.0 copy-start.4
  165.9 0.0 copy-start.2
  165.9 0.0 copy-start
  165.9 0.0 reduce-scatter.2.cloned.1.call-update
  166.0 0.0 all-gather.5.cloned.1.call-start
  166.0 698.9 %reduce-scatter.2.cloned.1.call-done = f32[24,768]{1,0:T(8,128)} async-done(((f32[1536,768]{1,0:T(8,128)}), f32[24,768]{1,0:T(8,128)}) %reduce-scatter.2.cloned.1.call-update) | async-done | bytes 73744 | tf_op jit(solution)/shard_map/reduce_scatter | solution.py:33
  864.9 1.5 multiply_reduce_fusion
  866.4 99.8 %psum.28 = f32[]{:T(128)} all-reduce(f32[]{:T(128)} %get-tuple-element.6), channel_id=1, replica_groups=mesh['dp'=64,'mp'=8] {'dp','mp'}, use_global_device_ids=true, to_apply=%region_2.3 | all-reduce | flops 1 | bytes 8 | tf_op jit(solution)/shard_map/psum | solution.py:45
  967.0 10.9 psum.29
  977.9 0.0 copy-done.4
  977.9 0.6 fusion.9
  978.5 0.0 copy-start.3
  978.5 142.6 %all-reduce = (f32[]{:T(128)}, f32[768]{0:T(1024)S(1)}) all-reduce(f32[]{:T(128)} %get-tuple-element.11, f32[768]{0:T(1024)S(1)} %get-tuple-element.4), channel_id=1, replica_groups=mesh['dp'=64,'mp'=8] {'dp'}, use_global_device_ids=true, to_apply=%region_8.9 | all-reduce | flops 769 | bytes 6152 | tf_op jit(solution)/shard_map/psum | solution.py:50
  1121.8 0.0 copy-done.2
  1121.8 0.0 copy-start.1
  1121.8 0.0 copy-done
  1121.8 1.6 fusion.8
  1123.5 0.0 all-gather.5.cloned.1.call-update
  1123.5 131.5 %all-gather.5.cloned.1.call-done = bf16[1536,768]{1,0:T(8,128)(2,1)} async-done(((bf16[24,768]{1,0:T(8,128)(2,1)}), bf16[1536,768]{1,0:T(8,128)(2,1)}) %all-gather.5.cloned.1.call-update) | async-done | bytes 2359312 | tf_op jit(solution)/shard_map/all_gather | solution.py:56
  1255.0 3.2 copy.14
  1258.2 0.0 copy-done.3
  1258.2 0.0 copy-done.1
  (3 shorter events, 0.0 us)
Async XLA Ops:
  7.2 150.7 %all-gather.3.cloned.1.call-start = ((), (), s32[]{:S(2)}) async-start(), calls=%async_computation.1 | async-start | bytes 2396160 | tf_op jit(solution)/shard_map/all_gather | solution.py:28
  8.7 856.1 %reduce-scatter.2.cloned.1.call-start = ((), (), s32[]{:S(2)}) async-start(), calls=%async_computation.2 | async-start | bytes 4792320 | tf_op jit(solution)/shard_map/reduce_scatter | solution.py:33
  165.9 812.0 %copy-start.4 = (f32[24]{0:T(128)S(1)}, f32[24]{0:T(128)}, u32[]{:S(2)}) copy-start(f32[24]{0:T(128)} %param.11) | copy-start | bytes 292
  165.9 955.9 %copy-start.2 = (f32[768]{0:T(1024)S(1)}, f32[768]{0:T(1024)}, u32[]{:S(2)}) copy-start(f32[768]{0:T(1024)} %param.12) | copy-start | bytes 9220
  165.9 955.9 %copy-start = (f32[24,768]{1,0:T(8,128)S(1)}, f32[24,768]{1,0:T(8,128)}, u32[]{:S(2)}) copy-start(f32[24,768]{1,0:T(8,128)} %param.10) | copy-start | bytes 221188
  166.0 1089.0 %all-gather.5.cloned.1.call-start = ((), (), s32[]{:S(2)}) async-start(), calls=%async_computation.3 | async-start | bytes 2396160 | tf_op jit(solution)/shard_map/all_gather | solution.py:56
  978.5 279.7 %copy-start.3 = (f32[24]{0:T(128)}, f32[24]{0:T(128)S(1)}, u32[]{:S(2)}) copy-start(f32[24]{0:T(128)S(1)} %get-tuple-element.18) | copy-start | bytes 292
  1121.8 136.4 %copy-start.1 = (f32[768]{0:T(1024)}, f32[768]{0:T(1024)S(1)}, u32[]{:S(2)}) copy-start(f32[768]{0:T(1024)S(1)} %multiply_add_fusion) | copy-start | bytes 9220
Sparse Core Ops, SparseCore 0:
  11.5 146.3 all-gather.2
  166.1 698.7 reduce-scatter.1
  1123.6 131.3 all-gather.4
where the time goes:
time: 1270 us; the launch traced here: 1260 us
  waiting for transfers between devices  978 us (77%)
  blocking collectives  253 us (20%)
  between operations  16.5 us (1%)
    reduce_scatter x1, waiting for transfers between devices, per_device(): lax.psum_scatter(lax.dot_general(masked, dpre, (((0,), (0,)), ((), ())),...  699 us
    all_gather x1, waiting for transfers between devices, per_device(): weight_full = lax.all_gather(weight_low, 'dp', axis=0, tiled=True)  148 us
    psum x1, blocking collectives, per_device(): row_mean = lax.psum(jnp.sum(row_state), 'dp') / D  143 us
    all_gather x1, waiting for transfers between devices, per_device(): lax.all_gather(new_master.astype(jnp.bfloat16), 'dp', axis=0, tiled=True)  131 us
    psum x1, blocking collectives, per_device(): total = lax.psum(norm_local, ('dp', 'mp'))  99.8 us
  transfers between devices with their start and end apart: 3, of which 3 were waited for; matrix products, arithmetic and copies ran while one was open for 0% of the time, Pallas kernels for 0%

commit v1 on v0

v1 whole, which is shorter than its diff:
```python
import functools

import jax
import jax.numpy as jnp
from jax import lax
from jax.experimental import pallas as pl
from jax.experimental.pallas import tpu as pltpu
from jax.sharding import PartitionSpec as P

D = 1536
FF = 6144
TMASK = 128
FMASK = 192
NX = 4
NZ = 16
NMP = 8
TOK = 512
ROWS = D // (NX * NZ)
COLS = FF // NMP
HALF = COLS // 2
BLOCK = ROWS * NZ

epsilon = 1e-06
decay_rate = 0.8
step_rate = 0.01

MESH = pl.DeviceIdType.MESH
F32 = jnp.float32
BF16 = jnp.bfloat16


def fold(rows):
    return jnp.concatenate([rows[:, :HALF], rows[:, HALF:]], axis=0)


class Gather:
    def __init__(self, buf, send_sem, recv_sem, x, z, mp):
        self.buf, self.send_sem, self.recv_sem = buf, send_sem, recv_sem
        self.x, self.z, self.mp = x, z, mp

    def copy(self, slot, k, x, z):
        return pltpu.make_async_remote_copy(
            src_ref=self.buf.at[slot],
            dst_ref=self.buf.at[slot],
            send_sem=self.send_sem.at[k],
            recv_sem=self.recv_sem.at[slot],
            device_id=(x * NZ + z, self.mp),
            device_id_type=MESH,
        )

    def slot(self, offset):
        return self.x * NZ + (self.z + offset) % NZ

    def arrived(self, slot):
        self.copy(slot, 0, self.x, self.z).wait_recv()

    def along_x(self, slot, k):
        for d in (1, 3, 2):
            self.copy(slot, k + d - 1, (self.x + d) % NX, self.z).start()

    def near(self, slot, k):
        for i, d in enumerate((2, 1, NZ - 1)):
            self.copy(slot, k + i, self.x, (self.z + d) % NZ).start()

    def start(self):
        own = self.slot(0)
        for i, d in enumerate((8, 4, 12)):
            self.copy(own, i, self.x, (self.z + d) % NZ).start()
        self.near(own, 3)
        self.along_x(own, 15)

    def forward(self):
        for i, d in enumerate((4, 12, 8)):
            slot = self.slot(d)
            self.arrived(slot)
            self.near(slot, 6 + 3 * i)
            self.along_x(slot, 18 + 3 * i)

        def step(t, _):
            far, m = t // 3, t % 3
            offset = 4 * far + 2 * m - 1 - 5 * (m // 2) + NZ
            slot = self.slot(offset)
            self.arrived(slot)
            self.along_x(slot, 27 + 3 * t)
            return 0

        lax.fori_loop(0, 12, step, 0)

    def wait_block(self, x):
        def step(i, _):
            self.arrived(x * NZ + i)
            return 0

        lax.fori_loop(0, NZ, step, 0)

    def finish(self):
        def step(k, _):
            self.copy(0, k, self.x, self.z).wait_send()
            return 0

        lax.fori_loop(0, NX * NZ - 1, step, 0)


def unfold_block(buf, out, x):
    def step(i, _):
        first = buf[x * NZ + 2 * i].astype(F32)
        second = buf[x * NZ + 2 * i + 1].astype(F32)
        rows = pl.ds(pl.multiple_of(x * BLOCK + i * 2 * ROWS, 2 * ROWS), 2 * ROWS)
        out[rows, :HALF] = jnp.concatenate([first[:ROWS], second[:ROWS]], axis=0).astype(BF16)
        out[rows, HALF:] = jnp.concatenate([first[ROWS:], second[ROWS:]], axis=0).astype(BF16)
        return 0

    lax.fori_loop(0, NZ // 2, step, 0)


def exchange(src, dst, send_sem, recv_sem, peers):
    copies = []
    for i, (to, send_at) in enumerate(peers):
        copies.append(
            pltpu.make_async_remote_copy(
                src_ref=src,
                dst_ref=dst.at[i],
                send_sem=send_sem.at[send_at],
                recv_sem=recv_sem.at[send_at],
                device_id=to,
                device_id_type=MESH,
            )
        )
    for copy in copies:
        copy.start()
    for copy in copies:
        copy.wait()


def kernel(
    frame_ref, chan_ref, feat_ref, master_ref, rmom_ref, cmom_ref, grad_ref,
    new_ref, rstate_ref, cstate_ref, low_ref,
    wbuf, weight, nbuf, masked, masked_t, pre, dpre,
    partial, xrecv, summed, lrecv, local, frecv,
    row_src, row_dst, vec, vec_x, vec_f, vec_l,
    ag_send, ag_recv, ag2_send, ag2_recv, rs_send, rs_recv, sc_send, sc_recv,
):
    dp, mp = lax.axis_index("dp"), lax.axis_index("mp")
    x, z = dp // NZ, dp % NZ

    def at(dx, dz):
        return (((x + dx) % NX) * NZ + (z + dz) % NZ, mp)

    x_peers = [at(d, 0) for d in (1, 2, 3)]
    far_peers = [at(0, d) for d in (4, 8, 12)]
    near_peers = [at(0, d) for d in (1, NZ - 1, 2)]
    mp_peers = [(dp, (mp + d) % NMP) for d in range(1, NMP)]

    own = pl.ds(0, ROWS)
    wbuf[dp] = fold(master_ref[own, :]).astype(BF16)

    barrier = pltpu.get_barrier_semaphore()
    greeted = x_peers + far_peers + near_peers + [at(0, NZ - 2)] + mp_peers
    for peer in greeted:
        pl.semaphore_signal(barrier, inc=1, device_id=peer, device_id_type=MESH)
    pl.semaphore_wait(barrier, len(greeted))

    gather = Gather(wbuf, ag_send, ag_recv, x, z, mp)
    gather.start()

    first_frame, first_chan = frame_ref[0], chan_ref[0]
    channel = lax.broadcasted_iota(jnp.int32, (1, D), 1)
    chan_keep = jnp.where((channel < first_chan) | (channel >= first_chan + FMASK), 1.0, 0.0)

    def mask_rows(i, _):
        rows = pl.ds(pl.multiple_of(i * 128, 128), 128)
        offset = lax.broadcasted_iota(jnp.int32, (128, 1), 0) + i * 128
        time_keep = jnp.where((offset < first_frame) | (offset >= first_frame + TMASK), 1.0, 0.0)
        kept = feat_ref[rows, :] * (time_keep * chan_keep).astype(BF16)
        masked[rows, :] = kept
        masked_t[:, rows] = kept.T
        return 0

    lax.fori_loop(0, TOK // 128, mask_rows, 0)

    gather.forward()

    for d in (0, 1, 3, 2):
        block = (x + d) % NX
        if d:
            gather.wait_block(block)
        unfold_block(wbuf, weight, block)
        depth = pl.ds(pl.multiple_of(block * BLOCK, BLOCK), BLOCK)

        def forward_tile(i, _, d=d, depth=depth):
            cols = pl.ds(pl.multiple_of(i * 256, 256), 256)
            term = jnp.dot(masked[:, depth], weight[depth, cols], preferred_element_type=F32)
            if d == 0:
                pre[:, cols] = term
            else:
                total = pre[:, cols] + term
                if d != 2:
                    pre[:, cols] = total
                else:
                    s = jax.nn.sigmoid(total)
                    slope = s + total * s * (1.0 - s)
                    dpre[:, cols] = (grad_ref[:, cols].astype(F32) * slope).astype(BF16)
            return 0

        lax.fori_loop(0, COLS // 256, forward_tile, 0)

    def x_copy(d, cls):
        i = (d - 1) * 4 + cls
        return pltpu.make_async_remote_copy(
            src_ref=partial.at[d, cls],
            dst_ref=xrecv.at[d - 1, cls],
            send_sem=rs_send.at[i],
            recv_sem=rs_recv.at[i],
            device_id=at(d, 0),
            device_id_type=MESH,
        )

    classes = [(z + d) % 4 for d in (2, 1, 3, 0)]
    for d in (2, 1, 3, 0):
        block = (x + d) % NX

        def grad_tile(i, _, d=d, block=block):
            rows = pl.ds(pl.multiple_of(block * BLOCK + i * 4 * ROWS, 32), 4 * ROWS)
            term = jnp.dot(masked_t[rows, :], dpre[...], preferred_element_type=F32)
            for j in range(4):
                partial[d, j, i] = term[j * ROWS : (j + 1) * ROWS]
            return 0

        lax.fori_loop(0, NZ // 4, grad_tile, 0)
        if d:
            for cls in classes:
                x_copy(d, cls).start()

    def near_copy(i):
        return pltpu.make_async_remote_copy(
            src_ref=summed.at[(near_peers[i][0]) % 4],
            dst_ref=lrecv.at[i],
            send_sem=rs_send.at[12 + i],
            recv_sem=rs_recv.at[12 + i],
            device_id=near_peers[i],
            device_id_type=MESH,
        )

    for n, cls in enumerate(classes):
        for d in (1, 3, 2):
            x_copy(d, cls).wait_recv()

        def add_x(j, _, cls=cls):
            summed[cls, j] = partial[0, cls, j] + xrecv[0, cls, j] + xrecv[1, cls, j] + xrecv[2, cls, j]
            return 0

        lax.fori_loop(0, 4, add_x, 0)
        if n < 3:
            near_copy((2, 0, 1)[n]).start()

    for i in (0, 1, 2):
        near_copy(i).wait_recv()
    mine = z % 4

    def far_copy(i):
        return pltpu.make_async_remote_copy(
            src_ref=local.at[(z // 4 + i + 1) % 4],
            dst_ref=frecv.at[i],
            send_sem=rs_send.at[15 + i],
            recv_sem=rs_recv.at[15 + i],
            device_id=far_peers[i],
            device_id_type=MESH,
        )

    for d in (2, 1, 3, 0):
        j = (z // 4 + d) % 4
        local[j] = summed[mine, j] + lrecv[0, j] + lrecv[1, j] + lrecv[2, j]
        if d:
            far_copy(d - 1).start()
    for i in (0, 1, 2):
        far_copy(i).wait_recv()
    grad = local[z // 4] + frecv[0] + frecv[1] + frecv[2]

    squared = grad * grad
    row_lanes = squared[:, :128]
    for i in range(1, COLS // 128):
        row_lanes = row_lanes + squared[:, i * 128 : (i + 1) * 128]
    row_src[...] = row_lanes
    exchange(row_src, row_dst, sc_send, sc_recv, [(p, i) for i, p in enumerate(mp_peers)])
    for i in range(NMP - 1):
        row_lanes = row_lanes + row_dst[i]
    row_total = jnp.sum(row_lanes, axis=1, keepdims=True)

    diag = lax.broadcasted_iota(jnp.int32, (ROWS, ROWS), 0) == lax.broadcasted_iota(jnp.int32, (ROWS, ROWS), 1)
    moment = jnp.sum(jnp.where(diag, rmom_ref[...], 0.0), axis=1, keepdims=True)
    column = jnp.sum(squared, axis=0, keepdims=True)
    pieces = [column[:, i * 128 : (i + 1) * 128] for i in range(COLS // 128)]
    pieces.append(jnp.sum(row_lanes, axis=0, keepdims=True))
    pieces.append(jnp.broadcast_to(jnp.sum(moment, axis=0, keepdims=True) * (1.0 / 128), (1, 128)))
    vec[0] = jnp.concatenate(pieces, axis=0)
    exchange(vec.at[0], vec_x, sc_send, sc_recv, [(p, 7 + i) for i, p in enumerate(x_peers)])
    vec[1] = vec[0] + vec_x[0] + vec_x[1] + vec_x[2]
    exchange(vec.at[1], vec_f, sc_send, sc_recv, [(p, 10 + i) for i, p in enumerate(far_peers)])
    vec[2] = vec[1] + vec_f[0] + vec_f[1] + vec_f[2]
    exchange(vec.at[2], vec_l, sc_send, sc_recv, [(p, 13 + i) for i, p in enumerate(near_peers)])
    sums = vec[2] + vec_l[0] + vec_l[1] + vec_l[2]
    col_total = jnp.concatenate([sums[i : i + 1] for i in range(COLS // 128)], axis=1)
    total = jnp.sum(sums[6:7], axis=1, keepdims=True)
    moments = jnp.sum(sums[7:8], axis=1, keepdims=True)

    clip = 1.0 / jnp.maximum(1.0, jnp.sqrt(total / (D * FF)))
    row_state = decay_rate * moment + (1.0 - decay_rate) * (clip * clip * row_total / FF + epsilon)
    col_state = decay_rate * cmom_ref[...] + (1.0 - decay_rate) * (clip * clip * col_total / D + epsilon)
    row_mean = decay_rate * moments / D + (1.0 - decay_rate) * (clip * clip * (total / FF) / D + epsilon)
    update = clip * grad * lax.rsqrt(row_state * col_state / row_mean)
    updated = master_ref[...] - step_rate * update
    nbuf[dp] = fold(updated).astype(BF16)

    regather = Gather(nbuf, ag2_send, ag2_recv, x, z, mp)
    regather.start()
    new_ref[...] = updated
    rstate_ref[...] = jnp.sum(jnp.where(diag, row_state, 0.0), axis=0, keepdims=True)
    cstate_ref[...] = col_state
    regather.forward()
    for d in (0, 1, 3, 2):
        block = (x + d) % NX
        if d:
            regather.wait_block(block)
        unfold_block(nbuf, low_ref, block)

    gather.finish()
    regather.finish()
    for d in (1, 2, 3):
        for cls in range(4):
            x_copy(d, cls).wait_send()
    for i in range(3):
        near_copy(i).wait_send()
        far_copy(i).wait_send()


def per_device(features, frame_start, chan_start, master_weight, row_moment, col_moment, out_grad):
    vmem = pl.BlockSpec(memory_space=pltpu.VMEM)
    smem = pl.BlockSpec(memory_space=pltpu.SMEM)
    new_master, row_state, col_state, compute_weight = pl.pallas_call(
        kernel,
        name="adafactor_step",
        out_shape=(
            jax.ShapeDtypeStruct((ROWS, COLS), F32),
            jax.ShapeDtypeStruct((1, ROWS), F32),
            jax.ShapeDtypeStruct((1, COLS), F32),
            jax.ShapeDtypeStruct((D, COLS), BF16),
        ),
        in_specs=[smem, smem, vmem, vmem, vmem, vmem, vmem],
        out_specs=(vmem, vmem, vmem, vmem),
        scratch_shapes=[
            pltpu.VMEM((NX * NZ, 2 * ROWS, HALF), BF16),
            pltpu.VMEM((D, COLS), BF16),
            pltpu.VMEM((NX * NZ, 2 * ROWS, HALF), BF16),
            pltpu.VMEM((TOK, D), BF16),
            pltpu.VMEM((D, TOK), BF16),
            pltpu.VMEM((TOK, COLS), F32),
            pltpu.VMEM((TOK, COLS), BF16),
            pltpu.VMEM((NX, 4, 4, ROWS, COLS), F32),
            pltpu.VMEM((NX - 1, 4, 4, ROWS, COLS), F32),
            pltpu.VMEM((4, 4, ROWS, COLS), F32),
            pltpu.VMEM((3, 4, ROWS, COLS), F32),
            pltpu.VMEM((4, ROWS, COLS), F32),
            pltpu.VMEM((3, ROWS, COLS), F32),
            pltpu.VMEM((ROWS, 128), F32),
            pltpu.VMEM((NMP - 1, ROWS, 128), F32),
            pltpu.VMEM((3, 8, 128), F32),
            pltpu.VMEM((3, 8, 128), F32),
            pltpu.VMEM((3, 8, 128), F32),
            pltpu.VMEM((3, 8, 128), F32),
            pltpu.SemaphoreType.DMA((NX * NZ,)),
            pltpu.SemaphoreType.DMA((NX * NZ,)),
            pltpu.SemaphoreType.DMA((NX * NZ,)),
            pltpu.SemaphoreType.DMA((NX * NZ,)),
            pltpu.SemaphoreType.DMA((18,)),
            pltpu.SemaphoreType.DMA((18,)),
            pltpu.SemaphoreType.DMA((16,)),
            pltpu.SemaphoreType.DMA((16,)),
        ],
        compiler_params=pltpu.CompilerParams(collective_id=0, has_side_effects=True, vmem_limit_bytes=56 * 2**20),
    )(
        frame_start, chan_start, features, master_weight, row_moment.reshape(1, ROWS), col_moment.reshape(1, COLS), out_grad
    )
    return new_master, row_state.reshape(ROWS), col_state.reshape(COLS), compute_weight


def solution(mesh):
    placed = (P("dp", None), P("dp"), P("dp"), P("dp", "mp"), P("dp"), P("mp"), P("dp", "mp"))
    return jax.shard_map(
        per_device,
        mesh=mesh,
        in_specs=placed,
        out_specs=(P("dp", "mp"), P("dp"), P("mp"), P(None, "mp")),
        check_vma=False,
    )
```

time: 1270 us -> 189 us (0.15)
  waiting for transfers between devices: 978 us -> 0 us
  blocking collectives: 253 us -> 0 us
  Pallas kernels: 0 us -> 177 us
  between operations: 16.5 us -> 1.94 us
    reduce_scatter x1 -> x0, waiting for transfers between devices: 699 us -> none  [per_device(): lax.psum_scatter(lax.dot_general(masked, dpre, (((0,), (0,)), ((), ())),...]
    all_gather x2 -> x0, waiting for transfers between devices: 279 us -> none  [the longest x1 148 us: per_device(): weight_full = lax.all_gather(weight_low, 'dp', axis=0, tiled=True)]
    psum x3 -> x0, blocking collectives: 253 us -> none  [the longest x1 143 us: per_device(): row_mean = lax.psum(jnp.sum(row_state), 'dp') / D]
    pallas_call x0 -> x1, Pallas kernels: none -> 177 us  [per_device(): pl.pallas_call(kernel, name='adafactor_step', out_shape=(jax.ShapeDtypeSt...]
  transfers between devices with their start and end apart: 3 -> 0, of which waited for: 3 -> 0; matrix products, arithmetic and copies ran while one was open for 0% -> 0% of each run, Pallas kernels for 0% -> 0%
where the time goes in v1:
time: 189 us; the launch traced here: 187 us
  Pallas kernels  177 us (94%)
  local copies, waits for them, and re-layouts  7.18 us (4%)
  between operations  1.94 us (1%)
    pallas_call x1, Pallas kernels, per_device(): pl.pallas_call(kernel, name='adafactor_step', out_shape=(jax.ShapeDtypeSt...  177 us
    unnamed x3, local copies, waits for them, and re-layouts  5.92 us

profile of v1, /device:TPU:24, one launch (start us, length us, event | category | flops | bytes accessed | tf_op | source)
XLA Modules:
  0.0 187.4 jit_solution(5542702734464959387)
XLA Ops:
  0.6 1.3 reshape.21.cmom_ref
  3.2 176.9 %adafactor_step.1 = (f32[24,768]{1,0:T(8,128)}, f32[1,24]{1,0:T(1,128)}, f32[1,768]{1,0:T(1,128)}, bf16[1536,768]{1,0:T(8,128)(2,1)}) custom-call(s32[1]{0:T(128)S(6)} %copy.14.frame_ref, s32[1]{0:T(128)S(6)} %copy.15.chan_ref, bf16[512,1536]{1,0:T(8,128)(2,1)} %feat_ref.1, f32[24,768]{1,0:T(8,128)} %master_ref.1, f32[1,24]{1,0:T(1,128)} %bitcast.2, ...), custom_call_target="tpu_custom_call" | custom-call | tf_op jit(solution)/shard_map/adafactor_step/pallas_call | solution.py:339
  180.1 1.3 reduce
  181.4 1.5 copy.16
  183.0 1.2 copy.17
  184.1 3.2 %copy.18 = bf16[1536,768]{1,0:T(8,128)(2,1)} copy(bf16[1536,768]{1,0:T(8,128)(2,1)} %get-tuple-element.19) | data formatting | bytes 4718592

commit v2 on v1

--- a/solution.py
+++ b/solution.py
@@ -27,6 +27,7 @@
 MESH = pl.DeviceIdType.MESH
 F32 = jnp.float32
 BF16 = jnp.bfloat16
+I16 = jnp.int16
 
 
 def fold(rows):
@@ -55,8 +56,8 @@
         self.copy(slot, 0, self.x, self.z).wait_recv()
 
     def along_x(self, slot, k):
-        for d in (1, 3, 2):
-            self.copy(slot, k + d - 1, (self.x + d) % NX, self.z).start()
+        for i, d in enumerate((1, NX - 1)):
+            self.copy(slot, k + i, (self.x + d) % NX, self.z).start()
 
     def near(self, slot, k):
         for i, d in enumerate((2, 1, NZ - 1)):
@@ -74,24 +75,41 @@
             slot = self.slot(d)
             self.arrived(slot)
             self.near(slot, 6 + 3 * i)
-            self.along_x(slot, 18 + 3 * i)
+            self.along_x(slot, 17 + 2 * i)
 
         def step(t, _):
             far, m = t // 3, t % 3
             offset = 4 * far + 2 * m - 1 - 5 * (m // 2) + NZ
             slot = self.slot(offset)
             self.arrived(slot)
-            self.along_x(slot, 27 + 3 * t)
+            self.along_x(slot, 23 + 2 * t)
             return 0
 
         lax.fori_loop(0, 12, step, 0)
 
-    def wait_block(self, x):
+        def relay(t, _):
+            far, n = t // 4, t % 4
+            owner = (self.z + 4 * far + (n // 2) * (1 - n % 2) - ((n + 1) // 2) * (n % 2) + NZ) % NZ
+            side = 1 - 2 * (owner % 2)
+            slot = ((self.x - side + NX) % NX) * NZ + owner
+            self.arrived(slot)
+            self.copy(slot, 47 + t, (self.x + side + NX) % NX, self.z).start()
+            return 0
+
+        lax.fori_loop(0, NZ, relay, 0)
+
+    def wait_block(self, d):
+        x = (self.x + d) % NX
+
         def step(i, _):
-            self.arrived(x * NZ + i)
+            if d == 2:
+                owner = i
+            else:
+                owner = 2 * i + (0 if d == 1 else 1)
+            self.arrived(x * NZ + owner)
             return 0
 
-        lax.fori_loop(0, NZ, step, 0)
+        lax.fori_loop(0, NZ if d == 2 else NZ // 2, step, 0)
 
     def finish(self):
         def step(k, _):
@@ -111,6 +129,36 @@
         return 0
 
     lax.fori_loop(0, NZ // 2, step, 0)
+
+
+def unfold(slot):
+    return jnp.concatenate([slot[:ROWS], slot[ROWS:]], axis=1)
+
+
+def pack(row):
+    pieces = [row[:, i * 128 : (i + 1) * 128] for i in range(COLS // 128)]
+    return jnp.concatenate(pieces + [jnp.zeros((8 - COLS // 128, 128), F32)], axis=0)
+
+
+def unpack(tile):
+    return jnp.concatenate([tile[i : i + 1] for i in range(COLS // 128)], axis=1)
+
+
+def peak_of(rows):
+    size = jnp.abs(rows)
+    return jnp.maximum(jnp.maximum(size[:8], size[8:16]), size[16:24])
+
+
+def scale_of(peak):
+    return jnp.maximum(jnp.max(peak, axis=0, keepdims=True), 1e-30)
+
+
+def encode(rows, inverse):
+    return jnp.round(fold(rows * inverse)).astype(jnp.int32).astype(I16)
+
+
+def decode(slot, scale):
+    return unfold(slot.astype(jnp.int32).astype(F32)) * scale
 
 
 def exchange(src, dst, send_sem, recv_sem, peers):
@@ -136,7 +184,7 @@
     frame_ref, chan_ref, feat_ref, master_ref, rmom_ref, cmom_ref, grad_ref,
     new_ref, rstate_ref, cstate_ref, low_ref,
     wbuf, weight, nbuf, masked, masked_t, pre, dpre,
-    partial, xrecv, summed, lrecv, local, frecv,
+    partial, coded, xrecv, summed, near_coded, lrecv, far_coded, frecv, scale_src, scale_dst,
     row_src, row_dst, vec, vec_x, vec_f, vec_l,
     ag_send, ag_recv, ag2_send, ag2_recv, rs_send, rs_recv, sc_send, sc_recv,
 ):
@@ -183,7 +231,7 @@
     for d in (0, 1, 3, 2):
         block = (x + d) % NX
         if d:
-            gather.wait_block(block)
+            gather.wait_block(d)
         unfold_block(wbuf, weight, block)
         depth = pl.ds(pl.multiple_of(block * BLOCK, BLOCK), BLOCK)
 
@@ -204,77 +252,112 @@
 
         lax.fori_loop(0, COLS // 256, forward_tile, 0)
 
-    def x_copy(d, cls):
-        i = (d - 1) * 4 + cls
+    def remote(src, dst, i, to):
         return pltpu.make_async_remote_copy(
-            src_ref=partial.at[d, cls],
-            dst_ref=xrecv.at[d - 1, cls],
+            src_ref=src,
+            dst_ref=dst,
             send_sem=rs_send.at[i],
             recv_sem=rs_recv.at[i],
-            device_id=at(d, 0),
+            device_id=to,
             device_id_type=MESH,
         )
+
+    def x_copy(d, cls):
+        return remote(coded.at[d - 1, cls], xrecv.at[d - 1, cls], (d - 1) * 4 + cls, at(d, 0))
+
+    def x_scale(d):
+        return remote(scale_src.at[d - 1], scale_dst.at[d - 1], 12 + d - 1, at(d, 0))
+
+    def near_copy(i):
+        return remote(near_coded.at[i], lrecv.at[i], 15 + i, near_peers[i])
+
+    def near_scale(i):
+        return remote(scale_src.at[3 + i], scale_dst.at[3 + i], 18 + i, near_peers[i])
+
+    def far_copy(i):
+        return remote(far_coded.at[i], frecv.at[i], 21 + i, far_peers[i])
+
+    def far_scale(i):
+        return remote(scale_src.at[6 + i], scale_dst.at[6 + i], 24 + i, far_peers[i])
 
     classes = [(z + d) % 4 for d in (2, 1, 3, 0)]
     for d in (2, 1, 3, 0):
         block = (x + d) % NX
-
-        def grad_tile(i, _, d=d, block=block):
+        held = 0 if d == 0 else 1
+
+        def grad_tile(i, peak, block=block, held=held):
             rows = pl.ds(pl.multiple_of(block * BLOCK + i * 4 * ROWS, 32), 4 * ROWS)
             term = jnp.dot(masked_t[rows, :], dpre[...], preferred_element_type=F32)
             for j in range(4):
-                partial[d, j, i] = term[j * ROWS : (j + 1) * ROWS]
-            return 0
-
-        lax.fori_loop(0, NZ // 4, grad_tile, 0)
+                slot = term[j * ROWS : (j + 1) * ROWS]
+                partial[held, j, i] = slot
+                peak = jnp.maximum(peak, peak_of(slot))
+            return peak
+
+        peak = lax.fori_loop(0, NZ // 4, grad_tile, jnp.zeros((8, COLS), F32))
         if d:
+            scale = scale_of(peak)
+            scale_src[d - 1] = pack(scale * (1.0 / 32767))
+            x_scale(d).start()
+            inverse = 32767.0 / scale
             for cls in classes:
+
+                def encode_slot(j, _, d=d, cls=cls, inverse=inverse):
+                    coded[d - 1, cls, j] = encode(partial[1, cls, j], inverse)
+                    return 0
+
+                lax.fori_loop(0, 4, encode_slot, 0)
                 x_copy(d, cls).start()
 
-    def near_copy(i):
-        return pltpu.make_async_remote_copy(
-            src_ref=summed.at[(near_peers[i][0]) % 4],
-            dst_ref=lrecv.at[i],
-            send_sem=rs_send.at[12 + i],
-            recv_sem=rs_recv.at[12 + i],
-            device_id=near_peers[i],
-            device_id_type=MESH,
-        )
-
+    for d in (1, 2, 3):
+        x_scale(d).wait_recv()
+    scales = [unpack(scale_dst[i]) for i in range(3)]
     for n, cls in enumerate(classes):
-        for d in (1, 3, 2):
+        for d in (2, 1, 3):
             x_copy(d, cls).wait_recv()
 
-        def add_x(j, _, cls=cls):
-            summed[cls, j] = partial[0, cls, j] + xrecv[0, cls, j] + xrecv[1, cls, j] + xrecv[2, cls, j]
-            return 0
-
-        lax.fori_loop(0, 4, add_x, 0)
+        def add_x(j, peak, cls=cls):
+            term = partial[0, cls, j]
+            for i in range(3):
+                term = term + decode(xrecv[i, cls, j], scales[i])
+            summed[j] = term
+            return jnp.maximum(peak, peak_of(term))
+
+        peak = lax.fori_loop(0, 4, add_x, jnp.zeros((8, COLS), F32))
         if n < 3:
-            near_copy((2, 0, 1)[n]).start()
-
+            i = (2, 0, 1)[n]
+            scale = scale_of(peak)
+            scale_src[3 + i] = pack(scale * (1.0 / 32767))
+            near_scale(i).start()
+            inverse = 32767.0 / scale
+
+            def encode_near(j, _, i=i, inverse=inverse):
+                near_coded[i, j] = encode(summed[j], inverse)
+                return 0
+
+            lax.fori_loop(0, 4, encode_near, 0)
+            near_copy(i).start()
+
+    for i in range(3):
+        near_scale(i).wait_recv()
+    scales = [unpack(scale_dst[3 + i]) for i in range(3)]
     for i in (0, 1, 2):
         near_copy(i).wait_recv()
-    mine = z % 4
-
-    def far_copy(i):
-        return pltpu.make_async_remote_copy(
-            src_ref=local.at[(z // 4 + i + 1) % 4],
-            dst_ref=frecv.at[i],
-            send_sem=rs_send.at[15 + i],
-            recv_sem=rs_recv.at[15 + i],
-            device_id=far_peers[i],
-            device_id_type=MESH,
-        )
-
     for d in (2, 1, 3, 0):
         j = (z // 4 + d) % 4
-        local[j] = summed[mine, j] + lrecv[0, j] + lrecv[1, j] + lrecv[2, j]
+        grad = summed[j]
+        for i in range(3):
+            grad = grad + decode(lrecv[i, j], scales[i])
         if d:
+            scale = scale_of(peak_of(grad))
+            scale_src[6 + d - 1] = pack(scale * (1.0 / 32767))
+            far_scale(d - 1).start()
+            far_coded[d - 1] = encode(grad, 32767.0 / scale)
             far_copy(d - 1).start()
-    for i in (0, 1, 2):
+    for i in range(3):
+        far_scale(i).wait_recv()
         far_copy(i).wait_recv()
-    grad = local[z // 4] + frecv[0] + frecv[1] + frecv[2]
+        grad = grad + decode(frecv[i], unpack(scale_dst[6 + i]))
 
     squared = grad * grad
     row_lanes = squared[:, :128]
@@ -299,7 +382,7 @@
     vec[2] = vec[1] + vec_f[0] + vec_f[1] + vec_f[2]
     exchange(vec.at[2], vec_l, sc_send, sc_recv, [(p, 13 + i) for i, p in enumerate(near_peers)])
     sums = vec[2] + vec_l[0] + vec_l[1] + vec_l[2]
-    col_total = jnp.concatenate([sums[i : i + 1] for i in range(COLS // 128)], axis=1)
+    col_total = unpack(sums)
     total = jnp.sum(sums[6:7], axis=1, keepdims=True)
     moments = jnp.sum(sums[7:8], axis=1, keepdims=True)
 
@@ -320,16 +403,19 @@
     for d in (0, 1, 3, 2):
         block = (x + d) % NX
         if d:
-            regather.wait_block(block)
+            regather.wait_block(d)
         unfold_block(nbuf, low_ref, block)
 
     gather.finish()
     regather.finish()
     for d in (1, 2, 3):
+        x_scale(d).wait_send()
         for cls in range(4):
             x_copy(d, cls).wait_send()
     for i in range(3):
+        near_scale(i).wait_send()
         near_copy(i).wait_send()
+        far_scale(i).wait_send()
         far_copy(i).wait_send()
 
 
@@ -355,12 +441,16 @@
             pltpu.VMEM((D, TOK), BF16),
             pltpu.VMEM((TOK, COLS), F32),
             pltpu.VMEM((TOK, COLS), BF16),
-            pltpu.VMEM((NX, 4, 4, ROWS, COLS), F32),
-            pltpu.VMEM((NX - 1, 4, 4, ROWS, COLS), F32),
-            pltpu.VMEM((4, 4, ROWS, COLS), F32),
-            pltpu.VMEM((3, 4, ROWS, COLS), F32),
+            pltpu.VMEM((2, 4, 4, ROWS, COLS), F32),
+            pltpu.VMEM((NX - 1, 4, 4, 2 * ROWS, HALF), I16),
+            pltpu.VMEM((NX - 1, 4, 4, 2 * ROWS, HALF), I16),
             pltpu.VMEM((4, ROWS, COLS), F32),
-            pltpu.VMEM((3, ROWS, COLS), F32),
+            pltpu.VMEM((3, 4, 2 * ROWS, HALF), I16),
+            pltpu.VMEM((3, 4, 2 * ROWS, HALF), I16),
+            pltpu.VMEM((3, 2 * ROWS, HALF), I16),
+            pltpu.VMEM((3, 2 * ROWS, HALF), I16),
+            pltpu.VMEM((9, 8, 128), F32),
+            pltpu.VMEM((9, 8, 128), F32),
             pltpu.VMEM((ROWS, 128), F32),
             pltpu.VMEM((NMP - 1, ROWS, 128), F32),
             pltpu.VMEM((3, 8, 128), F32),
@@ -371,8 +461,8 @@
             pltpu.SemaphoreType.DMA((NX * NZ,)),
             pltpu.SemaphoreType.DMA((NX * NZ,)),
             pltpu.SemaphoreType.DMA((NX * NZ,)),
-            pltpu.SemaphoreType.DMA((18,)),
-            pltpu.SemaphoreType.DMA((18,)),
+            pltpu.SemaphoreType.DMA((27,)),
+            pltpu.SemaphoreType.DMA((27,)),
             pltpu.SemaphoreType.DMA((16,)),
             pltpu.SemaphoreType.DMA((16,)),
         ],

time: 189 us -> 152 us (0.80)
  Pallas kernels: 177 us -> 140 us
    pallas_call x1, Pallas kernels: 177 us -> 140 us  [per_device(): pl.pallas_call(kernel, name='adafactor_step', out_shape=(jax.ShapeDtypeSt...]
where the time goes in v2:
time: 152 us; the launch traced here: 150 us
  Pallas kernels  140 us (92%)
  local copies, waits for them, and re-layouts  7.18 us (5%)
  between operations  1.94 us (1%)
    pallas_call x1, Pallas kernels, per_device(): pl.pallas_call(kernel, name='adafactor_step', out_shape=(jax.ShapeDtypeSt...  140 us
    unnamed x3, local copies, waits for them, and re-layouts  5.92 us

profile of v2, /device:TPU:24, one launch (start us, length us, event | category | flops | bytes accessed | tf_op | source)
XLA Modules:
  0.0 150.5 jit_solution(14837092588964199260)
XLA Ops:
  0.6 1.3 reshape.21.cmom_ref
  3.2 140.0 %adafactor_step.1 = (f32[24,768]{1,0:T(8,128)}, f32[1,24]{1,0:T(1,128)}, f32[1,768]{1,0:T(1,128)}, bf16[1536,768]{1,0:T(8,128)(2,1)}) custom-call(s32[1]{0:T(128)S(6)} %copy.14.frame_ref, s32[1]{0:T(128)S(6)} %copy.15.chan_ref, bf16[512,1536]{1,0:T(8,128)(2,1)} %feat_ref.1, f32[24,768]{1,0:T(8,128)} %master_ref.1, f32[1,24]{1,0:T(1,128)} %bitcast.2, ...), custom_call_target="tpu_custom_call" | custom-call | tf_op jit(solution)/shard_map/adafactor_step/pallas_call | solution.py:425
  143.3 1.3 reduce
  144.5 1.5 %copy.16 = f32[24,768]{1,0:T(8,128)} copy(f32[24,768]{1,0:T(8,128)} %get-tuple-element.16) | data formatting | bytes 147456
  146.1 1.2 copy.17
  147.2 3.2 %copy.18 = bf16[1536,768]{1,0:T(8,128)(2,1)} copy(bf16[1536,768]{1,0:T(8,128)(2,1)} %get-tuple-element.19) | data formatting | bytes 4718592

commit v3 on v2

--- a/solution.py
+++ b/solution.py
@@ -161,32 +161,13 @@
     return unfold(slot.astype(jnp.int32).astype(F32)) * scale
 
 
-def exchange(src, dst, send_sem, recv_sem, peers):
-    copies = []
-    for i, (to, send_at) in enumerate(peers):
-        copies.append(
-            pltpu.make_async_remote_copy(
-                src_ref=src,
-                dst_ref=dst.at[i],
-                send_sem=send_sem.at[send_at],
-                recv_sem=recv_sem.at[send_at],
-                device_id=to,
-                device_id_type=MESH,
-            )
-        )
-    for copy in copies:
-        copy.start()
-    for copy in copies:
-        copy.wait()
-
-
 def kernel(
-    frame_ref, chan_ref, feat_ref, master_ref, rmom_ref, cmom_ref, grad_ref,
-    new_ref, rstate_ref, cstate_ref, low_ref,
-    wbuf, weight, nbuf, masked, masked_t, pre, dpre,
+    frame_ref, chan_ref, feat_hbm, master_ref, rmom_ref, cmom_ref, grad_hbm,
+    new_ref, rstate_ref, cstate_ref, slots_ref,
+    wbuf, weight, nbuf, feat, grad_in, masked, masked_t, pre, dpre,
     partial, coded, xrecv, summed, near_coded, lrecv, far_coded, frecv, scale_src, scale_dst,
-    row_src, row_dst, vec, vec_x, vec_f, vec_l,
-    ag_send, ag_recv, ag2_send, ag2_recv, rs_send, rs_recv, sc_send, sc_recv,
+    row_src, row_dst, vec, vec_z, vec_p,
+    ag_send, ag_recv, ag2_send, ag2_recv, rs_send, rs_recv, row_send, row_recv, z_send, z_recv, p_send, p_recv, load_sem,
 ):
     dp, mp = lax.axis_index("dp"), lax.axis_index("mp")
     x, z = dp // NZ, dp % NZ
@@ -194,22 +175,32 @@
     def at(dx, dz):
         return (((x + dx) % NX) * NZ + (z + dz) % NZ, mp)
 
-    x_peers = [at(d, 0) for d in (1, 2, 3)]
+    near_peers = [at(0, d) for d in (1, NZ - 1, 2)]
     far_peers = [at(0, d) for d in (4, 8, 12)]
-    near_peers = [at(0, d) for d in (1, NZ - 1, 2)]
-    mp_peers = [(dp, (mp + d) % NMP) for d in range(1, NMP)]
-
-    own = pl.ds(0, ROWS)
-    wbuf[dp] = fold(master_ref[own, :]).astype(BF16)
+
+    def plane(i):
+        return (((x + i // NMP) % NX) * NZ + z, (mp + i % NMP) % NMP)
 
     barrier = pltpu.get_barrier_semaphore()
-    greeted = x_peers + far_peers + near_peers + [at(0, NZ - 2)] + mp_peers
-    for peer in greeted:
-        pl.semaphore_signal(barrier, inc=1, device_id=peer, device_id_type=MESH)
-    pl.semaphore_wait(barrier, len(greeted))
-
-    gather = Gather(wbuf, ag_send, ag_recv, x, z, mp)
-    gather.start()
+
+    def greet_z(d, _):
+        pl.semaphore_signal(barrier, inc=1, device_id=at(0, d), device_id_type=MESH)
+        return 0
+
+    def greet_plane(i, _):
+        pl.semaphore_signal(barrier, inc=1, device_id=plane(i), device_id_type=MESH)
+        return 0
+
+    lax.fori_loop(1, NZ, greet_z, 0)
+    lax.fori_loop(1, NX * NMP, greet_plane, 0)
+
+    load_feat = pltpu.make_async_copy(feat_hbm, feat, load_sem.at[0])
+    load_grad = pltpu.make_async_copy(grad_hbm, grad_in, load_sem.at[1])
+    load_feat.start()
+    load_grad.start()
+
+    wbuf[dp] = fold(master_ref[...]).astype(BF16)
+    load_feat.wait()
 
     first_frame, first_chan = frame_ref[0], chan_ref[0]
     channel = lax.broadcasted_iota(jnp.int32, (1, D), 1)
@@ -219,13 +210,20 @@
         rows = pl.ds(pl.multiple_of(i * 128, 128), 128)
         offset = lax.broadcasted_iota(jnp.int32, (128, 1), 0) + i * 128
         time_keep = jnp.where((offset < first_frame) | (offset >= first_frame + TMASK), 1.0, 0.0)
-        kept = feat_ref[rows, :] * (time_keep * chan_keep).astype(BF16)
+        kept = feat[rows, :] * (time_keep * chan_keep).astype(BF16)
         masked[rows, :] = kept
         masked_t[:, rows] = kept.T
         return 0
 
     lax.fori_loop(0, TOK // 128, mask_rows, 0)
-
+    pl.semaphore_wait(barrier, NZ - 1 + NX * NMP - 1)
+
+    gather = Gather(wbuf, ag_send, ag_recv, x, z, mp)
+    gather.start()
+    load_grad.wait()
+    diag = lax.broadcasted_iota(jnp.int32, (ROWS, ROWS), 0) == lax.broadcasted_iota(jnp.int32, (ROWS, ROWS), 1)
+    moment = jnp.sum(jnp.where(diag, rmom_ref[...].reshape(1, ROWS), 0.0), axis=1, keepdims=True)
+    moment_lanes = jnp.broadcast_to(jnp.sum(moment, axis=0, keepdims=True) * (1.0 / 128), (1, 128))
     gather.forward()
 
     for d in (0, 1, 3, 2):
@@ -247,7 +245,7 @@
                 else:
                     s = jax.nn.sigmoid(total)
                     slope = s + total * s * (1.0 - s)
-                    dpre[:, cols] = (grad_ref[:, cols].astype(F32) * slope).astype(BF16)
+                    dpre[:, cols] = (grad_in[:, cols].astype(F32) * slope).astype(BF16)
             return 0
 
         lax.fori_loop(0, COLS // 256, forward_tile, 0)
@@ -364,31 +362,71 @@
     for i in range(1, COLS // 128):
         row_lanes = row_lanes + squared[:, i * 128 : (i + 1) * 128]
     row_src[...] = row_lanes
-    exchange(row_src, row_dst, sc_send, sc_recv, [(p, i) for i, p in enumerate(mp_peers)])
+
+    def row_copy(i):
+        return pltpu.make_async_remote_copy(
+            src_ref=row_src,
+            dst_ref=row_dst.at[i - 1],
+            send_sem=row_send.at[i - 1],
+            recv_sem=row_recv.at[i - 1],
+            device_id=plane(i),
+            device_id_type=MESH,
+        )
+
+    def z_copy(d):
+        return pltpu.make_async_remote_copy(
+            src_ref=vec.at[0],
+            dst_ref=vec_z.at[d - 1],
+            send_sem=z_send.at[d - 1],
+            recv_sem=z_recv.at[d - 1],
+            device_id=at(0, d),
+            device_id_type=MESH,
+        )
+
+    def plane_copy(i):
+        return pltpu.make_async_remote_copy(
+            src_ref=vec.at[1],
+            dst_ref=vec_p.at[i - 1],
+            send_sem=p_send.at[i - 1],
+            recv_sem=p_recv.at[i - 1],
+            device_id=plane(i),
+            device_id_type=MESH,
+        )
+
+    def each(low, high, act):
+        def step(i, _):
+            act(i)
+            return 0
+
+        lax.fori_loop(low, high, step, 0)
+
+    column = jnp.sum(squared, axis=0, keepdims=True)
+    pieces = [column[:, i * 128 : (i + 1) * 128] for i in range(COLS // 128)]
+    pieces += [jnp.sum(row_lanes, axis=0, keepdims=True), moment_lanes]
+    vec[0] = jnp.concatenate(pieces, axis=0)
+    each(1, NZ, lambda d: z_copy((d * 7 + NZ) % NZ).start())
+    each(1, NMP, lambda i: row_copy(i).start())
+    each(1, NMP, lambda i: row_copy(i).wait_recv())
     for i in range(NMP - 1):
         row_lanes = row_lanes + row_dst[i]
     row_total = jnp.sum(row_lanes, axis=1, keepdims=True)
-
-    diag = lax.broadcasted_iota(jnp.int32, (ROWS, ROWS), 0) == lax.broadcasted_iota(jnp.int32, (ROWS, ROWS), 1)
-    moment = jnp.sum(jnp.where(diag, rmom_ref[...], 0.0), axis=1, keepdims=True)
-    column = jnp.sum(squared, axis=0, keepdims=True)
-    pieces = [column[:, i * 128 : (i + 1) * 128] for i in range(COLS // 128)]
-    pieces.append(jnp.sum(row_lanes, axis=0, keepdims=True))
-    pieces.append(jnp.broadcast_to(jnp.sum(moment, axis=0, keepdims=True) * (1.0 / 128), (1, 128)))
-    vec[0] = jnp.concatenate(pieces, axis=0)
-    exchange(vec.at[0], vec_x, sc_send, sc_recv, [(p, 7 + i) for i, p in enumerate(x_peers)])
-    vec[1] = vec[0] + vec_x[0] + vec_x[1] + vec_x[2]
-    exchange(vec.at[1], vec_f, sc_send, sc_recv, [(p, 10 + i) for i, p in enumerate(far_peers)])
-    vec[2] = vec[1] + vec_f[0] + vec_f[1] + vec_f[2]
-    exchange(vec.at[2], vec_l, sc_send, sc_recv, [(p, 13 + i) for i, p in enumerate(near_peers)])
-    sums = vec[2] + vec_l[0] + vec_l[1] + vec_l[2]
+    each(1, NZ, lambda d: z_copy(d).wait_recv())
+    sums = vec[0]
+    for i in range(NZ - 1):
+        sums = sums + vec_z[i]
+    vec[1] = sums
+    each(1, NX * NMP, lambda i: plane_copy(i).start())
+    each(1, NX * NMP, lambda i: plane_copy(i).wait_recv())
+    norm = sums[6:7] + jnp.sum(vec_p[:, 6, :], axis=0, keepdims=True)
+    for i in range(1, NX):
+        sums = sums + vec_p[NMP * i - 1]
     col_total = unpack(sums)
-    total = jnp.sum(sums[6:7], axis=1, keepdims=True)
+    total = jnp.sum(norm, axis=1, keepdims=True)
     moments = jnp.sum(sums[7:8], axis=1, keepdims=True)
 
     clip = 1.0 / jnp.maximum(1.0, jnp.sqrt(total / (D * FF)))
     row_state = decay_rate * moment + (1.0 - decay_rate) * (clip * clip * row_total / FF + epsilon)
-    col_state = decay_rate * cmom_ref[...] + (1.0 - decay_rate) * (clip * clip * col_total / D + epsilon)
+    col_state = decay_rate * cmom_ref[...].reshape(1, COLS) + (1.0 - decay_rate) * (clip * clip * col_total / D + epsilon)
     row_mean = decay_rate * moments / D + (1.0 - decay_rate) * (clip * clip * (total / FF) / D + epsilon)
     update = clip * grad * lax.rsqrt(row_state * col_state / row_mean)
     updated = master_ref[...] - step_rate * update
@@ -397,15 +435,21 @@
     regather = Gather(nbuf, ag2_send, ag2_recv, x, z, mp)
     regather.start()
     new_ref[...] = updated
-    rstate_ref[...] = jnp.sum(jnp.where(diag, row_state, 0.0), axis=0, keepdims=True)
-    cstate_ref[...] = col_state
+    rstate_ref[...] = jnp.sum(jnp.where(diag, row_state, 0.0), axis=0, keepdims=True).reshape(ROWS)
+    cstate_ref[...] = col_state.reshape(COLS)
     regather.forward()
+
+    def leave(d):
+        block = pl.ds(((x + d) % NX) * NZ, NZ)
+        return pltpu.make_async_copy(nbuf.at[block], slots_ref.at[block], load_sem.at[2 + d])
+
     for d in (0, 1, 3, 2):
-        block = (x + d) % NX
         if d:
             regather.wait_block(d)
-        unfold_block(nbuf, low_ref, block)
-
+        leave(d).start()
+    each(1, NMP, lambda i: row_copy(i).wait_send())
+    each(1, NZ, lambda d: z_copy(d).wait_send())
+    each(1, NX * NMP, lambda i: plane_copy(i).wait_send())
     gather.finish()
     regather.finish()
     for d in (1, 2, 3):
@@ -417,26 +461,45 @@
         near_copy(i).wait_send()
         far_scale(i).wait_send()
         far_copy(i).wait_send()
+    for d in range(NX):
+        leave(d).wait()
+
+
+def layout_kernel(slots, new_in, rstate_in, cstate_in, new_out, rstate_out, cstate_out, low):
+    @pl.when(pl.program_id(0) == 0)
+    def _():
+        new_out[...] = new_in[...]
+        rstate_out[...] = rstate_in[...]
+        cstate_out[...] = cstate_in[...]
+
+    for i in range(slots.shape[0] // 2):
+        first, second = slots[2 * i].astype(F32), slots[2 * i + 1].astype(F32)
+        rows = slice(2 * ROWS * i, 2 * ROWS * (i + 1))
+        low[rows, :HALF] = jnp.concatenate([first[:ROWS], second[:ROWS]], axis=0).astype(BF16)
+        low[rows, HALF:] = jnp.concatenate([first[ROWS:], second[ROWS:]], axis=0).astype(BF16)
 
 
 def per_device(features, frame_start, chan_start, master_weight, row_moment, col_moment, out_grad):
     vmem = pl.BlockSpec(memory_space=pltpu.VMEM)
     smem = pl.BlockSpec(memory_space=pltpu.SMEM)
-    new_master, row_state, col_state, compute_weight = pl.pallas_call(
+    small = (
+        jax.ShapeDtypeStruct((ROWS, COLS), F32),
+        jax.ShapeDtypeStruct((ROWS,), F32),
+        jax.ShapeDtypeStruct((COLS,), F32),
+    )
+    anywhere = pl.BlockSpec(memory_space=pl.ANY)
+    new_master, row_state, col_state, slots = pl.pallas_call(
         kernel,
         name="adafactor_step",
-        out_shape=(
-            jax.ShapeDtypeStruct((ROWS, COLS), F32),
-            jax.ShapeDtypeStruct((1, ROWS), F32),
-            jax.ShapeDtypeStruct((1, COLS), F32),
-            jax.ShapeDtypeStruct((D, COLS), BF16),
-        ),
-        in_specs=[smem, smem, vmem, vmem, vmem, vmem, vmem],
-        out_specs=(vmem, vmem, vmem, vmem),
+        out_shape=small + (jax.ShapeDtypeStruct((NX * NZ, 2 * ROWS, HALF), BF16),),
+        in_specs=[smem, smem, anywhere, vmem, vmem, vmem, anywhere],
+        out_specs=(vmem, vmem, vmem, anywhere),
         scratch_shapes=[
             pltpu.VMEM((NX * NZ, 2 * ROWS, HALF), BF16),
             pltpu.VMEM((D, COLS), BF16),
             pltpu.VMEM((NX * NZ, 2 * ROWS, HALF), BF16),
+            pltpu.VMEM((TOK, D), BF16),
+            pltpu.VMEM((TOK, COLS), BF16),
             pltpu.VMEM((TOK, D), BF16),
             pltpu.VMEM((D, TOK), BF16),
             pltpu.VMEM((TOK, COLS), F32),
@@ -453,24 +516,41 @@
             pltpu.VMEM((9, 8, 128), F32),
             pltpu.VMEM((ROWS, 128), F32),
             pltpu.VMEM((NMP - 1, ROWS, 128), F32),
-            pltpu.VMEM((3, 8, 128), F32),
-            pltpu.VMEM((3, 8, 128), F32),
-            pltpu.VMEM((3, 8, 128), F32),
-            pltpu.VMEM((3, 8, 128), F32),
+            pltpu.VMEM((2, 8, 128), F32),
+            pltpu.VMEM((NZ - 1, 8, 128), F32),
+            pltpu.VMEM((NX * NMP - 1, 8, 128), F32),
             pltpu.SemaphoreType.DMA((NX * NZ,)),
             pltpu.SemaphoreType.DMA((NX * NZ,)),
             pltpu.SemaphoreType.DMA((NX * NZ,)),
             pltpu.SemaphoreType.DMA((NX * NZ,)),
             pltpu.SemaphoreType.DMA((27,)),
             pltpu.SemaphoreType.DMA((27,)),
-            pltpu.SemaphoreType.DMA((16,)),
-            pltpu.SemaphoreType.DMA((16,)),
+            pltpu.SemaphoreType.DMA((NMP - 1,)),
+            pltpu.SemaphoreType.DMA((NMP - 1,)),
+            pltpu.SemaphoreType.DMA((NZ - 1,)),
+            pltpu.SemaphoreType.DMA((NZ - 1,)),
+            pltpu.SemaphoreType.DMA((NX * NMP - 1,)),
+            pltpu.SemaphoreType.DMA((NX * NMP - 1,)),
+            pltpu.SemaphoreType.DMA((2 + NX,)),
         ],
         compiler_params=pltpu.CompilerParams(collective_id=0, has_side_effects=True, vmem_limit_bytes=56 * 2**20),
-    )(
-        frame_start, chan_start, features, master_weight, row_moment.reshape(1, ROWS), col_moment.reshape(1, COLS), out_grad
+    )(frame_start, chan_start, features, master_weight, row_moment, col_moment, out_grad)
+
+    steps = 8
+    slots_step = NX * NZ // steps
+    whole = (
+        pl.BlockSpec((ROWS, COLS), lambda i: (0, 0)),
+        pl.BlockSpec((ROWS,), lambda i: (0,)),
+        pl.BlockSpec((COLS,), lambda i: (0,)),
     )
-    return new_master, row_state.reshape(ROWS), col_state.reshape(COLS), compute_weight
+    return pl.pallas_call(
+        layout_kernel,
+        name="layout",
+        grid=(steps,),
+        out_shape=small + (jax.ShapeDtypeStruct((D, COLS), BF16),),
+        in_specs=[pl.BlockSpec((slots_step, 2 * ROWS, HALF), lambda i: (i, 0, 0)), *whole],
+        out_specs=whole + (pl.BlockSpec((D // steps, COLS), lambda i: (i, 0)),),
+    )(slots, new_master, row_state, col_state)
 
 
 def solution(mesh):

time: 152 us -> 151 us (level)
  local copies, waits for them, and re-layouts: 7.18 us -> 0 us
  Pallas kernels: 140 us -> 147 us
    pallas_call x1 -> x2, Pallas kernels: 140 us -> 147 us  [the longest x1 141 us: per_device(): pl.pallas_call(kernel, name='adafactor_step', out_shape=small + (jax.Shap...]
    unnamed x3 -> x0, local copies, waits for them, and re-layouts: 5.92 us -> none
where the time goes in v3:
time: 151 us; the launch traced here: 149 us
  Pallas kernels  147 us (97%)
  between operations  1.93 us (1%)
    pallas_call x1, Pallas kernels, per_device(): pl.pallas_call(kernel, name='adafactor_step', out_shape=small + (jax.Shap...  141 us
    pallas_call x1, Pallas kernels, per_device(): pl.pallas_call(layout_kernel, name='layout', grid=(steps,), out_shape=sma...  5.87 us

profile of v3, /device:TPU:24, one launch (start us, length us, event | category | flops | bytes accessed | tf_op | source)
XLA Modules:
  0.0 149.0 jit_solution(8942645189391280870)
XLA Ops:
  1.9 141.2 %adafactor_step.1 = (f32[24,768]{1,0:T(8,128)}, f32[24]{0:T(128)}, f32[768]{0:T(1024)}, bf16[64,48,384]{2,1,0:T(8,128)(2,1)}) custom-call(s32[1]{0:T(128)S(6)} %copy.11.frame_ref, s32[1]{0:T(128)S(6)} %copy.12.chan_ref, bf16[512,1536]{1,0:T(8,128)(2,1)} %feat_hbm.1, f32[24,768]{1,0:T(8,128)} %master_ref.1, f32[24]{0:T(128)} %rmom_ref.1, f32[768]{0:T(1024)} %cmom_ref.1, ...), custom_call_target="tpu_custom_call" | custom-call | tf_op jit(solution)/shard_map/adafactor_step/pallas_call | solution.py:491
  143.2 5.9 %layout.1 = (f32[24,768]{1,0:T(8,128)}, f32[24]{0:T(128)}, f32[768]{0:T(1024)}, bf16[1536,768]{1,0:T(8,128)(2,1)}) custom-call(bf16[64,48,384]{2,1,0:T(8,128)(2,1)} %get-tuple-element.8.slots, f32[24,768]{1,0:T(8,128)} %get-tuple-element.9.new_in, f32[24]{0:T(128)} %get-tuple-element.10.rstate_in, f32[768]{0:T(1024)} %get-tuple-element.11.cstate_in), custom_call_target="tpu_custom_call" | custom-call | tf_op jit(solution)/shard_map/layout/pallas_call | solution.py:546

commit v4 on v3

--- a/solution.py
+++ b/solution.py
@@ -38,6 +38,12 @@
     def __init__(self, buf, send_sem, recv_sem, x, z, mp):
         self.buf, self.send_sem, self.recv_sem = buf, send_sem, recv_sem
         self.x, self.z, self.mp = x, z, mp
+        self.up, self.down = lax.rem(x + 1, NX), lax.rem(x + NX - 1, NX)
+        self.line = [lax.rem(z + o, NZ) for o in range(NZ)]
+        odd = lax.rem(z, 2)
+        self.relay_from = [self.down + (self.up - self.down) * p for p in (odd, 1 - odd)]
+        self.relay_to = [self.up + (self.down - self.up) * p for p in (odd, 1 - odd)]
+        self.sent = 0
 
     def copy(self, slot, k, x, z):
         return pltpu.make_async_remote_copy(
@@ -49,57 +55,64 @@
             device_id_type=MESH,
         )
 
-    def slot(self, offset):
-        return self.x * NZ + (self.z + offset) % NZ
+    def send(self, slot, x, z):
+        self.copy(slot, self.sent, x, z).start()
+        self.sent += 1
+
+    def slot(self, o):
+        return self.x * NZ + self.line[o]
 
     def arrived(self, slot):
         self.copy(slot, 0, self.x, self.z).wait_recv()
 
-    def along_x(self, slot, k):
-        for i, d in enumerate((1, NX - 1)):
-            self.copy(slot, k + i, (self.x + d) % NX, self.z).start()
-
-    def near(self, slot, k):
-        for i, d in enumerate((2, 1, NZ - 1)):
-            self.copy(slot, k + i, self.x, (self.z + d) % NZ).start()
+    def along_x(self, o):
+        self.send(self.slot(o), self.up, self.z)
+        self.send(self.slot(o), self.down, self.z)
+
+    def near(self, o):
+        for d in (2, 1, 15):
+            self.send(self.slot(o), self.x, self.line[d])
+
+    def relay(self, o):
+        slot = self.relay_from[o % 2] * NZ + self.line[o]
+        self.arrived(slot)
+        self.send(slot, self.relay_to[o % 2], self.z)
 
     def start(self):
-        own = self.slot(0)
-        for i, d in enumerate((8, 4, 12)):
-            self.copy(own, i, self.x, (self.z + d) % NZ).start()
-        self.near(own, 3)
-        self.along_x(own, 15)
+        for d in (8, 4, 12):
+            self.send(self.slot(0), self.x, self.line[d])
+        self.near(0)
+        self.along_x(0)
 
     def forward(self):
-        for i, d in enumerate((4, 12, 8)):
-            slot = self.slot(d)
-            self.arrived(slot)
-            self.near(slot, 6 + 3 * i)
-            self.along_x(slot, 17 + 2 * i)
-
-        def step(t, _):
-            far, m = t // 3, t % 3
-            offset = 4 * far + 2 * m - 1 - 5 * (m // 2) + NZ
-            slot = self.slot(offset)
-            self.arrived(slot)
-            self.along_x(slot, 23 + 2 * t)
-            return 0
-
-        lax.fori_loop(0, 12, step, 0)
-
-        def relay(t, _):
-            far, n = t // 4, t % 4
-            owner = (self.z + 4 * far + (n // 2) * (1 - n % 2) - ((n + 1) // 2) * (n % 2) + NZ) % NZ
-            side = 1 - 2 * (owner % 2)
-            slot = ((self.x - side + NX) % NX) * NZ + owner
-            self.arrived(slot)
-            self.copy(slot, 47 + t, (self.x + side + NX) % NX, self.z).start()
-            return 0
-
-        lax.fori_loop(0, NZ, relay, 0)
+        def far(o):
+            self.arrived(self.slot(o))
+            self.near(o)
+            self.along_x(o)
+
+        def pass_on(*offsets):
+            for o in offsets:
+                self.arrived(self.slot(o))
+                self.along_x(o)
+
+        def relay(*offsets):
+            for o in offsets:
+                self.relay(o)
+
+        pass_on(15, 1, 14)
+        relay(0)
+        far(4)
+        far(12)
+        relay(15, 1, 14)
+        far(8)
+        relay(4, 12)
+        pass_on(3, 5, 2, 11, 13, 10)
+        relay(8)
+        pass_on(7, 9, 6)
+        relay(3, 5, 2, 11, 13, 10, 7, 9, 6)
 
     def wait_block(self, d):
-        x = (self.x + d) % NX
+        x = lax.rem(self.x + d, NX)
 
         def step(i, _):
             if d == 2:
@@ -165,34 +178,27 @@
     frame_ref, chan_ref, feat_hbm, master_ref, rmom_ref, cmom_ref, grad_hbm,
     new_ref, rstate_ref, cstate_ref, slots_ref,
     wbuf, weight, nbuf, feat, grad_in, masked, masked_t, pre, dpre,
-    partial, coded, xrecv, summed, near_coded, lrecv, far_coded, frecv, scale_src, scale_dst,
+    partial, inverses, coded, xrecv, summed, near_coded, lrecv, far_coded, frecv, scale_src, scale_dst,
     row_src, row_dst, vec, vec_z, vec_p,
     ag_send, ag_recv, ag2_send, ag2_recv, rs_send, rs_recv, row_send, row_recv, z_send, z_recv, p_send, p_recv, load_sem,
 ):
     dp, mp = lax.axis_index("dp"), lax.axis_index("mp")
-    x, z = dp // NZ, dp % NZ
+    x, z = lax.div(dp, NZ), lax.rem(dp, NZ)
 
     def at(dx, dz):
-        return (((x + dx) % NX) * NZ + (z + dz) % NZ, mp)
+        return (lax.rem(x + dx, NX) * NZ + lax.rem(z + dz, NZ), mp)
 
     near_peers = [at(0, d) for d in (1, NZ - 1, 2)]
     far_peers = [at(0, d) for d in (4, 8, 12)]
 
     def plane(i):
-        return (((x + i // NMP) % NX) * NZ + z, (mp + i % NMP) % NMP)
+        return (lax.rem(x + i // NMP, NX) * NZ + z, lax.rem(mp + i % NMP, NMP))
 
     barrier = pltpu.get_barrier_semaphore()
 
-    def greet_z(d, _):
-        pl.semaphore_signal(barrier, inc=1, device_id=at(0, d), device_id_type=MESH)
-        return 0
-
-    def greet_plane(i, _):
-        pl.semaphore_signal(barrier, inc=1, device_id=plane(i), device_id_type=MESH)
-        return 0
-
-    lax.fori_loop(1, NZ, greet_z, 0)
-    lax.fori_loop(1, NX * NMP, greet_plane, 0)
+    greeted = [at(0, d) for d in range(1, NZ)] + [plane(i) for i in range(1, NX * NMP)]
+    for peer in greeted:
+        pl.semaphore_signal(barrier, inc=1, device_id=peer, device_id_type=MESH)
 
     load_feat = pltpu.make_async_copy(feat_hbm, feat, load_sem.at[0])
     load_grad = pltpu.make_async_copy(grad_hbm, grad_in, load_sem.at[1])
@@ -200,8 +206,11 @@
     load_grad.start()
 
     wbuf[dp] = fold(master_ref[...]).astype(BF16)
+    pl.semaphore_wait(barrier, len(greeted))
+    gather = Gather(wbuf, ag_send, ag_recv, x, z, mp)
+    gather.start()
+
     load_feat.wait()
-
     first_frame, first_chan = frame_ref[0], chan_ref[0]
     channel = lax.broadcasted_iota(jnp.int32, (1, D), 1)
     chan_keep = jnp.where((channel < first_chan) | (channel >= first_chan + FMASK), 1.0, 0.0)
@@ -216,10 +225,6 @@
         return 0
 
     lax.fori_loop(0, TOK // 128, mask_rows, 0)
-    pl.semaphore_wait(barrier, NZ - 1 + NX * NMP - 1)
-
-    gather = Gather(wbuf, ag_send, ag_recv, x, z, mp)
-    gather.start()
     load_grad.wait()
     diag = lax.broadcasted_iota(jnp.int32, (ROWS, ROWS), 0) == lax.broadcasted_iota(jnp.int32, (ROWS, ROWS), 1)
     moment = jnp.sum(jnp.where(diag, rmom_ref[...].reshape(1, ROWS), 0.0), axis=1, keepdims=True)
@@ -227,7 +232,7 @@
     gather.forward()
 
     for d in (0, 1, 3, 2):
-        block = (x + d) % NX
+        block = lax.rem(x + d, NX)
         if d:
             gather.wait_block(d)
         unfold_block(wbuf, weight, block)
@@ -278,17 +283,17 @@
     def far_scale(i):
         return remote(scale_src.at[6 + i], scale_dst.at[6 + i], 24 + i, far_peers[i])
 
-    classes = [(z + d) % 4 for d in (2, 1, 3, 0)]
-    for d in (2, 1, 3, 0):
-        block = (x + d) % NX
-        held = 0 if d == 0 else 1
-
-        def grad_tile(i, peak, block=block, held=held):
+    classes = [lax.rem(z + d, 4) for d in (2, 1, 3, 0)]
+
+    def grad_block(d):
+        block = lax.rem(x + d, NX)
+
+        def grad_tile(i, peak):
             rows = pl.ds(pl.multiple_of(block * BLOCK + i * 4 * ROWS, 32), 4 * ROWS)
             term = jnp.dot(masked_t[rows, :], dpre[...], preferred_element_type=F32)
             for j in range(4):
                 slot = term[j * ROWS : (j + 1) * ROWS]
-                partial[held, j, i] = slot
+                partial[d, j, i] = slot
                 peak = jnp.maximum(peak, peak_of(slot))
             return peak
 
@@ -297,15 +302,25 @@
             scale = scale_of(peak)
             scale_src[d - 1] = pack(scale * (1.0 / 32767))
             x_scale(d).start()
-            inverse = 32767.0 / scale
-            for cls in classes:
-
-                def encode_slot(j, _, d=d, cls=cls, inverse=inverse):
-                    coded[d - 1, cls, j] = encode(partial[1, cls, j], inverse)
-                    return 0
-
-                lax.fori_loop(0, 4, encode_slot, 0)
-                x_copy(d, cls).start()
+            inverses[d - 1] = jnp.broadcast_to(32767.0 / scale, (8, COLS))
+
+    def send_class(d, cls):
+        inverse = inverses[d - 1][:1]
+
+        def encode_slot(j, _):
+            coded[d - 1, cls, j] = encode(partial[d, cls, j], inverse)
+            return 0
+
+        lax.fori_loop(0, 4, encode_slot, 0)
+        x_copy(d, cls).start()
+
+    for d in (2, 1, 3):
+        grad_block(d)
+        send_class(d, classes[0])
+    grad_block(0)
+    for cls in classes[1:]:
+        for d in (2, 1, 3):
+            send_class(d, cls)
 
     for d in (1, 2, 3):
         x_scale(d).wait_recv()
@@ -342,7 +357,7 @@
     for i in (0, 1, 2):
         near_copy(i).wait_recv()
     for d in (2, 1, 3, 0):
-        j = (z // 4 + d) % 4
+        j = lax.rem(lax.div(z, 4) + d, 4)
         grad = summed[j]
         for i in range(3):
             grad = grad + decode(lrecv[i, j], scales[i])
@@ -394,17 +409,14 @@
         )
 
     def each(low, high, act):
-        def step(i, _):
+        for i in range(low, high):
             act(i)
-            return 0
-
-        lax.fori_loop(low, high, step, 0)
 
     column = jnp.sum(squared, axis=0, keepdims=True)
     pieces = [column[:, i * 128 : (i + 1) * 128] for i in range(COLS // 128)]
     pieces += [jnp.sum(row_lanes, axis=0, keepdims=True), moment_lanes]
     vec[0] = jnp.concatenate(pieces, axis=0)
-    each(1, NZ, lambda d: z_copy((d * 7 + NZ) % NZ).start())
+    each(1, NZ, lambda d: z_copy((d * 7) % NZ).start())
     each(1, NMP, lambda i: row_copy(i).start())
     each(1, NMP, lambda i: row_copy(i).wait_recv())
     for i in range(NMP - 1):
@@ -440,7 +452,7 @@
     regather.forward()
 
     def leave(d):
-        block = pl.ds(((x + d) % NX) * NZ, NZ)
+        block = pl.ds(lax.rem(x + d, NX) * NZ, NZ)
         return pltpu.make_async_copy(nbuf.at[block], slots_ref.at[block], load_sem.at[2 + d])
 
     for d in (0, 1, 3, 2):
@@ -504,7 +516,8 @@
             pltpu.VMEM((D, TOK), BF16),
             pltpu.VMEM((TOK, COLS), F32),
             pltpu.VMEM((TOK, COLS), BF16),
-            pltpu.VMEM((2, 4, 4, ROWS, COLS), F32),
+            pltpu.VMEM((NX, 4, 4, ROWS, COLS), F32),
+            pltpu.VMEM((NX - 1, 8, COLS), F32),
             pltpu.VMEM((NX - 1, 4, 4, 2 * ROWS, HALF), I16),
             pltpu.VMEM((NX - 1, 4, 4, 2 * ROWS, HALF), I16),
             pltpu.VMEM((4, ROWS, COLS), F32),
@@ -546,6 +559,7 @@
     return pl.pallas_call(
         layout_kernel,
         name="layout",
+        compiler_params=pltpu.CompilerParams(vmem_limit_bytes=60 * 2**20),
         grid=(steps,),
         out_shape=small + (jax.ShapeDtypeStruct((D, COLS), BF16),),
         in_specs=[pl.BlockSpec((slots_step, 2 * ROWS, HALF), lambda i: (i, 0, 0)), *whole],

time: 151 us -> 154 us (1.020)
  the two profiles are of different devices: /device:TPU:24 before, /device:TPU:2 now
where the time goes in v4:
time: 154 us
  Pallas kernels  152 us (99%)
  between operations  1.93 us (1%)
    pallas_call x1, Pallas kernels, per_device(): pl.pallas_call(kernel, name='adafactor_step', out_shape=small + (jax.Shap...  146 us
    pallas_call x1, Pallas kernels, per_device(): pl.pallas_call(layout_kernel, name='layout', compiler_params=pltpu.Compil...  5.87 us

profile of v4, /device:TPU:2, one launch (start us, length us, event | category | flops | bytes accessed | tf_op | source)
XLA Modules:
  0.0 153.9 jit_solution(10041517477538631084)
XLA Ops:
  1.9 146.1 %adafactor_step.1 = (f32[24,768]{1,0:T(8,128)}, f32[24]{0:T(128)}, f32[768]{0:T(1024)}, bf16[64,48,384]{2,1,0:T(8,128)(2,1)}) custom-call(s32[1]{0:T(128)S(6)} %copy.11.frame_ref, s32[1]{0:T(128)S(6)} %copy.12.chan_ref, bf16[512,1536]{1,0:T(8,128)(2,1)} %feat_hbm.1, f32[24,768]{1,0:T(8,128)} %master_ref.1, f32[24]{0:T(128)} %rmom_ref.1, f32[768]{0:T(1024)} %cmom_ref.1, ...), custom_call_target="tpu_custom_call" | custom-call | tf_op jit(solution)/shard_map/adafactor_step/pallas_call | solution.py:503
  148.1 5.9 %layout.1 = (f32[24,768]{1,0:T(8,128)}, f32[24]{0:T(128)}, f32[768]{0:T(1024)}, bf16[1536,768]{1,0:T(8,128)(2,1)}) custom-call(bf16[64,48,384]{2,1,0:T(8,128)(2,1)} %get-tuple-element.8.slots, f32[24,768]{1,0:T(8,128)} %get-tuple-element.9.new_in, f32[24]{0:T(128)} %get-tuple-element.10.rstate_in, f32[768]{0:T(1024)} %get-tuple-element.11.cstate_in), custom_call_target="tpu_custom_call" | custom-call | tf_op jit(solution)/shard_map/layout/pallas_call | solution.py:559

commit v5 on v4

--- a/solution.py
+++ b/solution.py
@@ -84,32 +84,36 @@
         self.near(0)
         self.along_x(0)
 
-    def forward(self):
-        def far(o):
+    def far(self, o):
+        self.arrived(self.slot(o))
+        self.near(o)
+        self.along_x(o)
+
+    def pass_on(self, *offsets):
+        for o in offsets:
             self.arrived(self.slot(o))
-            self.near(o)
             self.along_x(o)
 
-        def pass_on(*offsets):
-            for o in offsets:
-                self.arrived(self.slot(o))
-                self.along_x(o)
-
-        def relay(*offsets):
-            for o in offsets:
-                self.relay(o)
-
-        pass_on(15, 1, 14)
-        relay(0)
-        far(4)
-        far(12)
-        relay(15, 1, 14)
-        far(8)
-        relay(4, 12)
-        pass_on(3, 5, 2, 11, 13, 10)
-        relay(8)
-        pass_on(7, 9, 6)
-        relay(3, 5, 2, 11, 13, 10, 7, 9, 6)
+    def relays(self, *offsets):
+        for o in offsets:
+            self.relay(o)
+
+    def events(self):
+        self.pass_on(15, 1, 14)
+        self.relays(0)
+        yield
+        self.far(4)
+        self.far(12)
+        self.relays(15, 1, 14)
+        self.far(8)
+        self.relays(4, 12)
+        yield
+        self.pass_on(3, 5, 2, 11, 13, 10)
+        self.relays(8)
+        self.pass_on(7, 9, 6)
+        yield
+        self.relays(3, 5, 2, 11, 13, 10, 7, 9, 6)
+        yield
 
     def wait_block(self, d):
         x = lax.rem(self.x + d, NX)
@@ -132,25 +136,70 @@
         lax.fori_loop(0, NX * NZ - 1, step, 0)
 
 
-def unfold_block(buf, out, x):
-    def step(i, _):
-        first = buf[x * NZ + 2 * i].astype(F32)
-        second = buf[x * NZ + 2 * i + 1].astype(F32)
-        rows = pl.ds(pl.multiple_of(x * BLOCK + i * 2 * ROWS, 2 * ROWS), 2 * ROWS)
-        out[rows, :HALF] = jnp.concatenate([first[:ROWS], second[:ROWS]], axis=0).astype(BF16)
-        out[rows, HALF:] = jnp.concatenate([first[ROWS:], second[ROWS:]], axis=0).astype(BF16)
-        return 0
-
-    lax.fori_loop(0, NZ // 2, step, 0)
+class Tiles:
+    def __init__(self, buf, send_sem, recv_sem, x, z, mp):
+        self.buf, self.send_sem, self.recv_sem = buf, send_sem, recv_sem
+        self.x, self.z, self.mp = x, z, mp
+        self.sent = []
+
+    def index(self, x, z):
+        return x * NZ + lax.rem(z, 4) * 4 + lax.div(z, 4)
+
+    def round(self, first, count, k, peers):
+        for i, peer in enumerate(peers):
+            block = self.buf.at[pl.ds(first, count)]
+            copy = pltpu.make_async_remote_copy(
+                src_ref=block,
+                dst_ref=block,
+                send_sem=self.send_sem.at[k + i],
+                recv_sem=self.recv_sem.at[k + i],
+                device_id=peer,
+                device_id_type=MESH,
+            )
+            copy.start()
+            self.sent.append(copy)
+
+    def arrived(self, k):
+        for copy in self.sent[k : k + 3]:
+            copy.wait_recv()
+
+    def along(self, distances):
+        return [(self.x * NZ + lax.rem(self.z + d, NZ), self.mp) for d in distances]
+
+    def far(self):
+        self.round(self.index(self.x, self.z), 1, 0, self.along((8, 4, 12)))
+
+    def near(self):
+        self.arrived(0)
+        self.round(self.x * NZ + lax.rem(self.z, 4) * 4, 4, 3, self.along((2, 1, 15)))
+
+    def across(self):
+        self.arrived(3)
+        peers = [(lax.rem(self.x + d, NX) * NZ + self.z, self.mp) for d in (2, 1, 3)]
+        self.round(self.x * NZ, NZ, 6, peers)
+
+    def finish(self):
+        for copy in self.sent:
+            copy.wait_send()
+
+
+def stack(first, second):
+    return jnp.concatenate([first, second], axis=0).astype(BF16)
 
 
 def unfold(slot):
     return jnp.concatenate([slot[:ROWS], slot[ROWS:]], axis=1)
 
 
-def pack(row):
-    pieces = [row[:, i * 128 : (i + 1) * 128] for i in range(COLS // 128)]
-    return jnp.concatenate(pieces + [jnp.zeros((8 - COLS // 128, 128), F32)], axis=0)
+def pack(row, *more):
+    pieces = [row[:, i * 128 : (i + 1) * 128] for i in range(COLS // 128)] + list(more)
+    if len(pieces) < 8:
+        pieces.append(jnp.zeros((8 - len(pieces), 128), F32))
+    return jnp.concatenate(pieces, axis=0)
+
+
+def raw(slot):
+    return unfold(slot.astype(jnp.int32).astype(F32))
 
 
 def unpack(tile):
@@ -171,16 +220,16 @@
 
 
 def decode(slot, scale):
-    return unfold(slot.astype(jnp.int32).astype(F32)) * scale
+    return raw(slot) * scale
 
 
 def kernel(
     frame_ref, chan_ref, feat_hbm, master_ref, rmom_ref, cmom_ref, grad_hbm,
-    new_ref, rstate_ref, cstate_ref, slots_ref,
-    wbuf, weight, nbuf, feat, grad_in, masked, masked_t, pre, dpre,
+    new_ref, rstate_ref, cstate_ref, low_ref,
+    wbuf, wtile, weight, nbuf, ntile, low, feat, grad_in, masked, masked_t, pre, dpre,
     partial, inverses, coded, xrecv, summed, near_coded, lrecv, far_coded, frecv, scale_src, scale_dst,
     row_src, row_dst, vec, vec_z, vec_p,
-    ag_send, ag_recv, ag2_send, ag2_recv, rs_send, rs_recv, row_send, row_recv, z_send, z_recv, p_send, p_recv, load_sem,
+    ag_send, ag_recv, ag2_send, ag2_recv, rs_send, rs_recv, row_send, row_recv, z_send, z_recv, p_send, p_recv, wt_send, wt_recv, nt_send, nt_recv, load_sem,
 ):
     dp, mp = lax.axis_index("dp"), lax.axis_index("mp")
     x, z = lax.div(dp, NZ), lax.rem(dp, NZ)
@@ -205,8 +254,23 @@
     load_feat.start()
     load_grad.start()
 
-    wbuf[dp] = fold(master_ref[...]).astype(BF16)
+    master = master_ref[...]
+    peak = scale_of(peak_of(master))
+    diag = lax.broadcasted_iota(jnp.int32, (ROWS, 128), 0) == lax.broadcasted_iota(jnp.int32, (ROWS, 128), 1)
+
+    def to_lanes(column):
+        return jnp.sum(jnp.where(diag, column, 0.0), axis=0, keepdims=True)
+
+    def to_rows(lanes):
+        return jnp.sum(jnp.where(diag, lanes, 0.0), axis=1, keepdims=True)
+
+    moment_lanes = jnp.concatenate([rmom_ref[...].reshape(1, ROWS), jnp.zeros((1, 128 - ROWS), F32)], axis=1)
+    wbuf[dp] = encode(master, 32767.0 / peak)
+    tiles = Tiles(wtile, wt_send, wt_recv, x, z, mp)
+    wtile[tiles.index(x, z)] = pack(peak * (1.0 / 32767), moment_lanes)
+
     pl.semaphore_wait(barrier, len(greeted))
+    tiles.far()
     gather = Gather(wbuf, ag_send, ag_recv, x, z, mp)
     gather.start()
 
@@ -226,16 +290,32 @@
 
     lax.fori_loop(0, TOK // 128, mask_rows, 0)
     load_grad.wait()
-    diag = lax.broadcasted_iota(jnp.int32, (ROWS, ROWS), 0) == lax.broadcasted_iota(jnp.int32, (ROWS, ROWS), 1)
-    moment = jnp.sum(jnp.where(diag, rmom_ref[...].reshape(1, ROWS), 0.0), axis=1, keepdims=True)
-    moment_lanes = jnp.broadcast_to(jnp.sum(moment, axis=0, keepdims=True) * (1.0 / 128), (1, 128))
-    gather.forward()
+    moment = to_rows(moment_lanes)
+    for part, _ in enumerate(gather.events()):
+        if part == 1:
+            tiles.near()
+        elif part == 2:
+            tiles.across()
+    tiles.arrived(6)
+
+    def weights(slot):
+        tile = wtile[tiles.index(lax.div(slot, NZ), lax.rem(slot, NZ))]
+        return decode(wbuf[slot], unpack(tile)), tile
+
+    def weight_block(block):
+        def step(i, _):
+            slot = block * NZ + 2 * i
+            rows = pl.ds(pl.multiple_of(slot * ROWS, 2 * ROWS), 2 * ROWS)
+            weight[rows, :] = stack(weights(slot)[0], weights(slot + 1)[0])
+            return 0
+
+        lax.fori_loop(0, NZ // 2, step, 0)
 
     for d in (0, 1, 3, 2):
         block = lax.rem(x + d, NX)
         if d:
             gather.wait_block(d)
-        unfold_block(wbuf, weight, block)
+        weight_block(block)
         depth = pl.ds(pl.multiple_of(block * BLOCK, BLOCK), BLOCK)
 
         def forward_tile(i, _, d=d, depth=depth):
@@ -372,6 +452,10 @@
         far_copy(i).wait_recv()
         grad = grad + decode(frecv[i], unpack(scale_dst[6 + i]))
 
+    peak = scale_of(peak_of(grad))
+    nbuf[dp] = encode(grad, 32767.0 / peak)
+    regather = Gather(nbuf, ag2_send, ag2_recv, x, z, mp)
+    regather.start()
     squared = grad * grad
     row_lanes = squared[:, :128]
     for i in range(1, COLS // 128):
@@ -413,21 +497,32 @@
             act(i)
 
     column = jnp.sum(squared, axis=0, keepdims=True)
-    pieces = [column[:, i * 128 : (i + 1) * 128] for i in range(COLS // 128)]
-    pieces += [jnp.sum(row_lanes, axis=0, keepdims=True), moment_lanes]
-    vec[0] = jnp.concatenate(pieces, axis=0)
+    vec[0] = pack(column, jnp.sum(row_lanes, axis=0, keepdims=True), moment_lanes)
+    each(1, NMP, lambda i: row_copy(i).start())
     each(1, NZ, lambda d: z_copy((d * 7) % NZ).start())
-    each(1, NMP, lambda i: row_copy(i).start())
+    events = regather.events()
+    next(events)
+
     each(1, NMP, lambda i: row_copy(i).wait_recv())
     for i in range(NMP - 1):
         row_lanes = row_lanes + row_dst[i]
     row_total = jnp.sum(row_lanes, axis=1, keepdims=True)
+    retiles = Tiles(ntile, nt_send, nt_recv, x, z, mp)
+    ntile[retiles.index(x, z)] = pack(peak * (1.0 / 32767), to_lanes(row_total))
+    retiles.far()
+    next(events)
+
     each(1, NZ, lambda d: z_copy(d).wait_recv())
     sums = vec[0]
     for i in range(NZ - 1):
         sums = sums + vec_z[i]
     vec[1] = sums
     each(1, NX * NMP, lambda i: plane_copy(i).start())
+    retiles.near()
+    next(events)
+    retiles.across()
+    next(events)
+
     each(1, NX * NMP, lambda i: plane_copy(i).wait_recv())
     norm = sums[6:7] + jnp.sum(vec_p[:, 6, :], axis=0, keepdims=True)
     for i in range(1, NX):
@@ -437,28 +532,44 @@
     moments = jnp.sum(sums[7:8], axis=1, keepdims=True)
 
     clip = 1.0 / jnp.maximum(1.0, jnp.sqrt(total / (D * FF)))
-    row_state = decay_rate * moment + (1.0 - decay_rate) * (clip * clip * row_total / FF + epsilon)
+
+    def next_row_state(old, squares):
+        return decay_rate * old + (1.0 - decay_rate) * (clip * clip * squares / FF + epsilon)
+
+    row_state = next_row_state(moment, row_total)
     col_state = decay_rate * cmom_ref[...].reshape(1, COLS) + (1.0 - decay_rate) * (clip * clip * col_total / D + epsilon)
     row_mean = decay_rate * moments / D + (1.0 - decay_rate) * (clip * clip * (total / FF) / D + epsilon)
-    update = clip * grad * lax.rsqrt(row_state * col_state / row_mean)
-    updated = master_ref[...] - step_rate * update
-    nbuf[dp] = fold(updated).astype(BF16)
-
-    regather = Gather(nbuf, ag2_send, ag2_recv, x, z, mp)
-    regather.start()
-    new_ref[...] = updated
-    rstate_ref[...] = jnp.sum(jnp.where(diag, row_state, 0.0), axis=0, keepdims=True).reshape(ROWS)
+    col_factor = step_rate * clip * lax.rsqrt(col_state)
+    new_ref[...] = master_ref[...] - grad * (lax.rsqrt(row_state / row_mean) * col_factor)
+    rstate_ref[...] = to_lanes(row_state)[:, :ROWS].reshape(ROWS)
     cstate_ref[...] = col_state.reshape(COLS)
-    regather.forward()
+    retiles.arrived(6)
+
+    def updated(slot):
+        old, tile = weights(slot)
+        retile = ntile[retiles.index(lax.div(slot, NZ), lax.rem(slot, NZ))]
+        row_factor = to_rows(lax.rsqrt(next_row_state(tile[6:7], retile[6:7]) / row_mean))
+        return old - raw(nbuf[slot]) * (unpack(retile) * col_factor) * row_factor
 
     def leave(d):
-        block = pl.ds(lax.rem(x + d, NX) * NZ, NZ)
-        return pltpu.make_async_copy(nbuf.at[block], slots_ref.at[block], load_sem.at[2 + d])
+        rows = pl.ds(pl.multiple_of(lax.rem(x + d, NX) * BLOCK, BLOCK), BLOCK)
+        return pltpu.make_async_copy(low.at[rows], low_ref.at[rows], load_sem.at[2 + d])
 
     for d in (0, 1, 3, 2):
+        block = lax.rem(x + d, NX)
         if d:
             regather.wait_block(d)
+
+        def update_pair(i, _, block=block):
+            slot = block * NZ + 2 * i
+            rows = pl.ds(pl.multiple_of(slot * ROWS, 2 * ROWS), 2 * ROWS)
+            low[rows, :] = stack(updated(slot), updated(slot + 1))
+            return 0
+
+        lax.fori_loop(0, NZ // 2, update_pair, 0)
         leave(d).start()
+    tiles.finish()
+    retiles.finish()
     each(1, NMP, lambda i: row_copy(i).wait_send())
     each(1, NZ, lambda d: z_copy(d).wait_send())
     each(1, NX * NMP, lambda i: plane_copy(i).wait_send())
@@ -477,39 +588,39 @@
         leave(d).wait()
 
 
-def layout_kernel(slots, new_in, rstate_in, cstate_in, new_out, rstate_out, cstate_out, low):
-    @pl.when(pl.program_id(0) == 0)
-    def _():
-        new_out[...] = new_in[...]
-        rstate_out[...] = rstate_in[...]
-        cstate_out[...] = cstate_in[...]
-
-    for i in range(slots.shape[0] // 2):
-        first, second = slots[2 * i].astype(F32), slots[2 * i + 1].astype(F32)
-        rows = slice(2 * ROWS * i, 2 * ROWS * (i + 1))
-        low[rows, :HALF] = jnp.concatenate([first[:ROWS], second[:ROWS]], axis=0).astype(BF16)
-        low[rows, HALF:] = jnp.concatenate([first[ROWS:], second[ROWS:]], axis=0).astype(BF16)
+def copy_kernel(*refs):
+    count = len(refs) // 2
+    sources, targets, sem = refs[:count], refs[count : 2 * count], refs[-1]
+    copies = [pltpu.make_async_copy(a, b, sem.at[i]) for i, (a, b) in enumerate(zip(sources, targets))]
+    for copy in copies:
+        copy.start()
+    for copy in copies:
+        copy.wait()
 
 
 def per_device(features, frame_start, chan_start, master_weight, row_moment, col_moment, out_grad):
     vmem = pl.BlockSpec(memory_space=pltpu.VMEM)
     smem = pl.BlockSpec(memory_space=pltpu.SMEM)
-    small = (
+    out_shape = (
         jax.ShapeDtypeStruct((ROWS, COLS), F32),
         jax.ShapeDtypeStruct((ROWS,), F32),
         jax.ShapeDtypeStruct((COLS,), F32),
+        jax.ShapeDtypeStruct((D, COLS), BF16),
     )
     anywhere = pl.BlockSpec(memory_space=pl.ANY)
-    new_master, row_state, col_state, slots = pl.pallas_call(
+    results = pl.pallas_call(
         kernel,
         name="adafactor_step",
-        out_shape=small + (jax.ShapeDtypeStruct((NX * NZ, 2 * ROWS, HALF), BF16),),
+        out_shape=out_shape,
         in_specs=[smem, smem, anywhere, vmem, vmem, vmem, anywhere],
         out_specs=(vmem, vmem, vmem, anywhere),
         scratch_shapes=[
-            pltpu.VMEM((NX * NZ, 2 * ROWS, HALF), BF16),
+            pltpu.VMEM((NX * NZ, 2 * ROWS, HALF), I16),
+            pltpu.VMEM((NX * NZ, 8, 128), F32),
             pltpu.VMEM((D, COLS), BF16),
-            pltpu.VMEM((NX * NZ, 2 * ROWS, HALF), BF16),
+            pltpu.VMEM((NX * NZ, 2 * ROWS, HALF), I16),
+            pltpu.VMEM((NX * NZ, 8, 128), F32),
+            pltpu.VMEM((D, COLS), BF16),
             pltpu.VMEM((TOK, D), BF16),
             pltpu.VMEM((TOK, COLS), BF16),
             pltpu.VMEM((TOK, D), BF16),
@@ -544,27 +655,24 @@
             pltpu.SemaphoreType.DMA((NZ - 1,)),
             pltpu.SemaphoreType.DMA((NX * NMP - 1,)),
             pltpu.SemaphoreType.DMA((NX * NMP - 1,)),
+            pltpu.SemaphoreType.DMA((9,)),
+            pltpu.SemaphoreType.DMA((9,)),
+            pltpu.SemaphoreType.DMA((9,)),
+            pltpu.SemaphoreType.DMA((9,)),
             pltpu.SemaphoreType.DMA((2 + NX,)),
         ],
         compiler_params=pltpu.CompilerParams(collective_id=0, has_side_effects=True, vmem_limit_bytes=56 * 2**20),
     )(frame_start, chan_start, features, master_weight, row_moment, col_moment, out_grad)
 
-    steps = 8
-    slots_step = NX * NZ // steps
-    whole = (
-        pl.BlockSpec((ROWS, COLS), lambda i: (0, 0)),
-        pl.BlockSpec((ROWS,), lambda i: (0,)),
-        pl.BlockSpec((COLS,), lambda i: (0,)),
-    )
     return pl.pallas_call(
-        layout_kernel,
-        name="layout",
+        copy_kernel,
+        name="results",
+        out_shape=out_shape,
+        in_specs=[anywhere] * 4,
+        out_specs=(anywhere,) * 4,
+        scratch_shapes=[pltpu.SemaphoreType.DMA((4,))],
         compiler_params=pltpu.CompilerParams(vmem_limit_bytes=60 * 2**20),
-        grid=(steps,),
-        out_shape=small + (jax.ShapeDtypeStruct((D, COLS), BF16),),
-        in_specs=[pl.BlockSpec((slots_step, 2 * ROWS, HALF), lambda i: (i, 0, 0)), *whole],
-        out_specs=whole + (pl.BlockSpec((D // steps, COLS), lambda i: (i, 0)),),
-    )(slots, new_master, row_state, col_state)
+    )(*results)
 
 
 def solution(mesh):

time: 154 us -> 214 us (1.39)
  the two profiles are of different devices: /device:TPU:2 before, /device:TPU:24 now
where the time goes in v5:
time: 214 us
  Pallas kernels  212 us (99%)
    pallas_call x1, Pallas kernels, per_device(): pl.pallas_call(kernel, name='adafactor_step', out_shape=out_shape, in_spe...  137 us
    pallas_call x1, Pallas kernels, per_device(): pl.pallas_call(copy_kernel, name='results', out_shape=out_shape, in_specs...  75 us

profile of v5, /device:TPU:24, one launch (start us, length us, event | category | flops | bytes accessed | tf_op | source)
XLA Modules:
  0.0 214.3 jit_solution(12918781676818244051)
XLA Ops:
  1.9 137.4 %adafactor_step.1 = (f32[24,768]{1,0:T(8,128)}, f32[24]{0:T(128)}, f32[768]{0:T(1024)}, bf16[1536,768]{1,0:T(8,128)(2,1)}) custom-call(s32[1]{0:T(128)S(6)} %copy.11.frame_ref, s32[1]{0:T(128)S(6)} %copy.12.chan_ref, bf16[512,1536]{1,0:T(8,128)(2,1)} %feat_hbm.1, f32[24,768]{1,0:T(8,128)} %master_ref.1, f32[24]{0:T(128)} %rmom_ref.1, f32[768]{0:T(1024)} %cmom_ref.1, ...), custom_call_target="tpu_custom_call" | custom-call | tf_op jit(solution)/shard_map/adafactor_step/pallas_call | solution.py:611
  139.3 75.0 %results.1 = (f32[24,768]{1,0:T(8,128)}, f32[24]{0:T(128)}, f32[768]{0:T(1024)}, bf16[1536,768]{1,0:T(8,128)(2,1)}) custom-call(f32[24,768]{1,0:T(8,128)} %get-tuple-element.8.refs_0_, f32[24]{0:T(128)} %get-tuple-element.9.refs_1_, f32[768]{0:T(1024)} %get-tuple-element.10.refs_2_, bf16[1536,768]{1,0:T(8,128)(2,1)} %get-tuple-element.11.refs_3_), custom_call_target="tpu_custom_call" | custom-call | tf_op jit(solution)/shard_map/results/pallas_call | solution.py:667

commit v6 on v5

--- a/solution.py
+++ b/solution.py
@@ -255,7 +255,7 @@
     load_grad.start()
 
     master = master_ref[...]
-    peak = scale_of(peak_of(master))
+    peak = jnp.max(scale_of(peak_of(master)), axis=1, keepdims=True)
     diag = lax.broadcasted_iota(jnp.int32, (ROWS, 128), 0) == lax.broadcasted_iota(jnp.int32, (ROWS, 128), 1)
 
     def to_lanes(column):
@@ -265,9 +265,10 @@
         return jnp.sum(jnp.where(diag, lanes, 0.0), axis=1, keepdims=True)
 
     moment_lanes = jnp.concatenate([rmom_ref[...].reshape(1, ROWS), jnp.zeros((1, 128 - ROWS), F32)], axis=1)
+    lane = lax.broadcasted_iota(jnp.int32, (1, 128), 1)
     wbuf[dp] = encode(master, 32767.0 / peak)
     tiles = Tiles(wtile, wt_send, wt_recv, x, z, mp)
-    wtile[tiles.index(x, z)] = pack(peak * (1.0 / 32767), moment_lanes)
+    wtile[tiles.index(x, z)] = jnp.where(lane == 127, peak * (1.0 / 32767), moment_lanes)
 
     pl.semaphore_wait(barrier, len(greeted))
     tiles.far()
@@ -300,7 +301,7 @@
 
     def weights(slot):
         tile = wtile[tiles.index(lax.div(slot, NZ), lax.rem(slot, NZ))]
-        return decode(wbuf[slot], unpack(tile)), tile
+        return decode(wbuf[slot], tile[:, 127:128]), tile
 
     def weight_block(block):
         def step(i, _):
@@ -546,9 +547,9 @@
     retiles.arrived(6)
 
     def updated(slot):
-        old, tile = weights(slot)
+        old, old_moment = weights(slot)
         retile = ntile[retiles.index(lax.div(slot, NZ), lax.rem(slot, NZ))]
-        row_factor = to_rows(lax.rsqrt(next_row_state(tile[6:7], retile[6:7]) / row_mean))
+        row_factor = to_rows(lax.rsqrt(next_row_state(old_moment, retile[6:7]) / row_mean))
         return old - raw(nbuf[slot]) * (unpack(retile) * col_factor) * row_factor
 
     def leave(d):
@@ -588,13 +589,19 @@
         leave(d).wait()
 
 
-def copy_kernel(*refs):
-    count = len(refs) // 2
-    sources, targets, sem = refs[:count], refs[count : 2 * count], refs[-1]
-    copies = [pltpu.make_async_copy(a, b, sem.at[i]) for i, (a, b) in enumerate(zip(sources, targets))]
-    for copy in copies:
+def copy_kernel(new_in, rstate_in, cstate_in, low_in, new_out, rstate_out, cstate_out, low_out, new, rstate, cstate, low, sem):
+    pieces = 4
+    size = D // pieces
+    ways = [(low_in.at[pl.ds(i * size, size)], low.at[pl.ds(i * size, size)], low_out.at[pl.ds(i * size, size)]) for i in range(pieces)]
+    ways += [(new_in, new, new_out), (rstate_in, rstate, rstate_out), (cstate_in, cstate, cstate_out)]
+    come = [pltpu.make_async_copy(a, b, sem.at[0, i]) for i, (a, b, _) in enumerate(ways)]
+    go = [pltpu.make_async_copy(b, c, sem.at[1, i]) for i, (_, b, c) in enumerate(ways)]
+    for copy in come:
         copy.start()
-    for copy in copies:
+    for first, second in zip(come, go):
+        first.wait()
+        second.start()
+    for copy in go:
         copy.wait()
 
 
@@ -616,7 +623,7 @@
         out_specs=(vmem, vmem, vmem, anywhere),
         scratch_shapes=[
             pltpu.VMEM((NX * NZ, 2 * ROWS, HALF), I16),
-            pltpu.VMEM((NX * NZ, 8, 128), F32),
+            pltpu.VMEM((NX * NZ, 1, 128), F32),
             pltpu.VMEM((D, COLS), BF16),
             pltpu.VMEM((NX * NZ, 2 * ROWS, HALF), I16),
             pltpu.VMEM((NX * NZ, 8, 128), F32),
@@ -670,7 +677,7 @@
         out_shape=out_shape,
         in_specs=[anywhere] * 4,
         out_specs=(anywhere,) * 4,
-        scratch_shapes=[pltpu.SemaphoreType.DMA((4,))],
+        scratch_shapes=[pltpu.VMEM(out.shape, out.dtype) for out in out_shape] + [pltpu.SemaphoreType.DMA((2, 7))],
         compiler_params=pltpu.CompilerParams(vmem_limit_bytes=60 * 2**20),
     )(*results)
 

time: 214 us -> 139 us (0.65)
  Pallas kernels: 212 us -> 137 us
    pallas_call x1, Pallas kernels: 75 us -> 2.6 us  [per_device(): pl.pallas_call(copy_kernel, name='results', out_shape=out_shape, in_specs...]
    pallas_call x1, Pallas kernels: 137 us -> 134 us  [per_device(): pl.pallas_call(kernel, name='adafactor_step', out_shape=out_shape, in_spe...]
where the time goes in v6:
time: 139 us
  Pallas kernels  137 us (99%)
  between operations  1.93 us (1%)
    pallas_call x1, Pallas kernels, per_device(): pl.pallas_call(kernel, name='adafactor_step', out_shape=out_shape, in_spe...  134 us

profile of v6, /device:TPU:24, one launch (start us, length us, event | category | flops | bytes accessed | tf_op | source)
XLA Modules:
  0.0 138.8 jit_solution(9751859935651642809)
XLA Ops:
  1.9 134.2 %adafactor_step.1 = (f32[24,768]{1,0:T(8,128)}, f32[24]{0:T(128)}, f32[768]{0:T(1024)}, bf16[1536,768]{1,0:T(8,128)(2,1)}) custom-call(s32[1]{0:T(128)S(6)} %copy.11.frame_ref, s32[1]{0:T(128)S(6)} %copy.12.chan_ref, bf16[512,1536]{1,0:T(8,128)(2,1)} %feat_hbm.1, f32[24,768]{1,0:T(8,128)} %master_ref.1, f32[24]{0:T(128)} %rmom_ref.1, f32[768]{0:T(1024)} %cmom_ref.1, ...), custom_call_target="tpu_custom_call" | custom-call | tf_op jit(solution)/shard_map/adafactor_step/pallas_call | solution.py:618
  136.2 2.6 %results.1 = (f32[24,768]{1,0:T(8,128)}, f32[24]{0:T(128)}, f32[768]{0:T(1024)}, bf16[1536,768]{1,0:T(8,128)(2,1)}) custom-call(f32[24,768]{1,0:T(8,128)} %get-tuple-element.8.new_in, f32[24]{0:T(128)} %get-tuple-element.9.rstate_in, f32[768]{0:T(1024)} %get-tuple-element.10.cstate_in, bf16[1536,768]{1,0:T(8,128)(2,1)} %get-tuple-element.11.low_in), custom_call_target="tpu_custom_call" | custom-call | tf_op jit(solution)/shard_map/results/pallas_call | solution.py:674

commit v7 on v6

--- a/solution.py
+++ b/solution.py
@@ -228,8 +228,8 @@
     new_ref, rstate_ref, cstate_ref, low_ref,
     wbuf, wtile, weight, nbuf, ntile, low, feat, grad_in, masked, masked_t, pre, dpre,
     partial, inverses, coded, xrecv, summed, near_coded, lrecv, far_coded, frecv, scale_src, scale_dst,
-    row_src, row_dst, vec, vec_z, vec_p,
-    ag_send, ag_recv, ag2_send, ag2_recv, rs_send, rs_recv, row_send, row_recv, z_send, z_recv, p_send, p_recv, wt_send, wt_recv, nt_send, nt_recv, load_sem,
+    row_src, row_dst, vec, vec_in,
+    ag_send, ag_recv, ag2_send, ag2_recv, rs_send, rs_recv, row_send, row_recv, vec_send, vec_recv, wt_send, wt_recv, nt_send, nt_recv, load_sem,
 ):
     dp, mp = lax.axis_index("dp"), lax.axis_index("mp")
     x, z = lax.div(dp, NZ), lax.rem(dp, NZ)
@@ -237,15 +237,13 @@
     def at(dx, dz):
         return (lax.rem(x + dx, NX) * NZ + lax.rem(z + dz, NZ), mp)
 
+    x_peers = [at(d, 0) for d in (1, 2, 3)]
     near_peers = [at(0, d) for d in (1, NZ - 1, 2)]
     far_peers = [at(0, d) for d in (4, 8, 12)]
-
-    def plane(i):
-        return (lax.rem(x + i // NMP, NX) * NZ + z, lax.rem(mp + i % NMP, NMP))
+    mp_peers = [(dp, lax.rem(mp + d, NMP)) for d in range(1, NMP)]
 
     barrier = pltpu.get_barrier_semaphore()
-
-    greeted = [at(0, d) for d in range(1, NZ)] + [plane(i) for i in range(1, NX * NMP)]
+    greeted = far_peers + near_peers + [at(0, NZ - 2)] + x_peers + mp_peers
     for peer in greeted:
         pl.semaphore_signal(barrier, inc=1, device_id=peer, device_id_type=MESH)
 
@@ -293,9 +291,9 @@
     load_grad.wait()
     moment = to_rows(moment_lanes)
     for part, _ in enumerate(gather.events()):
-        if part == 1:
+        if part == 2:
             tiles.near()
-        elif part == 2:
+        elif part == 3:
             tiles.across()
     tiles.arrived(6)
 
@@ -466,70 +464,63 @@
     def row_copy(i):
         return pltpu.make_async_remote_copy(
             src_ref=row_src,
-            dst_ref=row_dst.at[i - 1],
-            send_sem=row_send.at[i - 1],
-            recv_sem=row_recv.at[i - 1],
-            device_id=plane(i),
+            dst_ref=row_dst.at[i],
+            send_sem=row_send.at[i],
+            recv_sem=row_recv.at[i],
+            device_id=mp_peers[i],
             device_id_type=MESH,
         )
 
-    def z_copy(d):
+    def vec_copy(step, i):
         return pltpu.make_async_remote_copy(
-            src_ref=vec.at[0],
-            dst_ref=vec_z.at[d - 1],
-            send_sem=z_send.at[d - 1],
-            recv_sem=z_recv.at[d - 1],
-            device_id=at(0, d),
+            src_ref=vec.at[step],
+            dst_ref=vec_in.at[step, i],
+            send_sem=vec_send.at[step, i],
+            recv_sem=vec_recv.at[step, i],
+            device_id=(x_peers, far_peers, near_peers)[step][i],
             device_id_type=MESH,
         )
 
-    def plane_copy(i):
-        return pltpu.make_async_remote_copy(
-            src_ref=vec.at[1],
-            dst_ref=vec_p.at[i - 1],
-            send_sem=p_send.at[i - 1],
-            recv_sem=p_recv.at[i - 1],
-            device_id=plane(i),
-            device_id_type=MESH,
-        )
-
-    def each(low, high, act):
-        for i in range(low, high):
-            act(i)
-
+    def vec_start(step):
+        for i in range(3):
+            vec_copy(step, i).start()
+
+    def vec_sum(step):
+        sums = vec[step]
+        for i in range(3):
+            vec_copy(step, i).wait_recv()
+            sums = sums + vec_in[step, i]
+        return sums
+
+    for i in range(NMP - 1):
+        row_copy(i).start()
     column = jnp.sum(squared, axis=0, keepdims=True)
-    vec[0] = pack(column, jnp.sum(row_lanes, axis=0, keepdims=True), moment_lanes)
-    each(1, NMP, lambda i: row_copy(i).start())
-    each(1, NZ, lambda d: z_copy((d * 7) % NZ).start())
     events = regather.events()
     next(events)
 
-    each(1, NMP, lambda i: row_copy(i).wait_recv())
     for i in range(NMP - 1):
+        row_copy(i).wait_recv()
         row_lanes = row_lanes + row_dst[i]
+    vec[0] = pack(column, jnp.sum(row_lanes, axis=0, keepdims=True), moment_lanes)
+    vec_start(0)
     row_total = jnp.sum(row_lanes, axis=1, keepdims=True)
     retiles = Tiles(ntile, nt_send, nt_recv, x, z, mp)
     ntile[retiles.index(x, z)] = pack(peak * (1.0 / 32767), to_lanes(row_total))
     retiles.far()
     next(events)
 
-    each(1, NZ, lambda d: z_copy(d).wait_recv())
-    sums = vec[0]
-    for i in range(NZ - 1):
-        sums = sums + vec_z[i]
-    vec[1] = sums
-    each(1, NX * NMP, lambda i: plane_copy(i).start())
+    vec[1] = vec_sum(0)
+    vec_start(1)
+    next(events)
+    vec[2] = vec_sum(1)
+    vec_start(2)
     retiles.near()
     next(events)
     retiles.across()
-    next(events)
-
-    each(1, NX * NMP, lambda i: plane_copy(i).wait_recv())
-    norm = sums[6:7] + jnp.sum(vec_p[:, 6, :], axis=0, keepdims=True)
-    for i in range(1, NX):
-        sums = sums + vec_p[NMP * i - 1]
+
+    sums = vec_sum(2)
     col_total = unpack(sums)
-    total = jnp.sum(norm, axis=1, keepdims=True)
+    total = jnp.sum(sums[6:7], axis=1, keepdims=True)
     moments = jnp.sum(sums[7:8], axis=1, keepdims=True)
 
     clip = 1.0 / jnp.maximum(1.0, jnp.sqrt(total / (D * FF)))
@@ -571,9 +562,11 @@
         leave(d).start()
     tiles.finish()
     retiles.finish()
-    each(1, NMP, lambda i: row_copy(i).wait_send())
-    each(1, NZ, lambda d: z_copy(d).wait_send())
-    each(1, NX * NMP, lambda i: plane_copy(i).wait_send())
+    for i in range(NMP - 1):
+        row_copy(i).wait_send()
+    for step in range(3):
+        for i in range(3):
+            vec_copy(step, i).wait_send()
     gather.finish()
     regather.finish()
     for d in (1, 2, 3):
@@ -647,9 +640,8 @@
             pltpu.VMEM((9, 8, 128), F32),
             pltpu.VMEM((ROWS, 128), F32),
             pltpu.VMEM((NMP - 1, ROWS, 128), F32),
-            pltpu.VMEM((2, 8, 128), F32),
-            pltpu.VMEM((NZ - 1, 8, 128), F32),
-            pltpu.VMEM((NX * NMP - 1, 8, 128), F32),
+            pltpu.VMEM((3, 8, 128), F32),
+            pltpu.VMEM((3, 3, 8, 128), F32),
             pltpu.SemaphoreType.DMA((NX * NZ,)),
             pltpu.SemaphoreType.DMA((NX * NZ,)),
             pltpu.SemaphoreType.DMA((NX * NZ,)),
@@ -658,10 +650,8 @@
             pltpu.SemaphoreType.DMA((27,)),
             pltpu.SemaphoreType.DMA((NMP - 1,)),
             pltpu.SemaphoreType.DMA((NMP - 1,)),
-            pltpu.SemaphoreType.DMA((NZ - 1,)),
-            pltpu.SemaphoreType.DMA((NZ - 1,)),
-            pltpu.SemaphoreType.DMA((NX * NMP - 1,)),
-            pltpu.SemaphoreType.DMA((NX * NMP - 1,)),
+            pltpu.SemaphoreType.DMA((3, 3)),
+            pltpu.SemaphoreType.DMA((3, 3)),
             pltpu.SemaphoreType.DMA((9,)),
             pltpu.SemaphoreType.DMA((9,)),
             pltpu.SemaphoreType.DMA((9,)),

time: 139 us -> 143 us (1.029)
  Pallas kernels: 137 us -> 140 us
    pallas_call x1, Pallas kernels: 134 us -> 137 us  [per_device(): pl.pallas_call(kernel, name='adafactor_step', out_shape=out_shape, in_spe...]
where the time goes in v7:
time: 143 us; the launch traced here: 142 us
  Pallas kernels  140 us (98%)
  between operations  1.93 us (1%)
    pallas_call x1, Pallas kernels, per_device(): pl.pallas_call(kernel, name='adafactor_step', out_shape=out_shape, in_spe...  137 us

profile of v7, /device:TPU:24, one launch (start us, length us, event | category | flops | bytes accessed | tf_op | source)
XLA Modules:
  0.0 141.5 jit_solution(16228946277666732425)
XLA Ops:
  1.9 137.0 %adafactor_step.1 = (f32[24,768]{1,0:T(8,128)}, f32[24]{0:T(128)}, f32[768]{0:T(1024)}, bf16[1536,768]{1,0:T(8,128)(2,1)}) custom-call(s32[1]{0:T(128)S(6)} %copy.11.frame_ref, s32[1]{0:T(128)S(6)} %copy.12.chan_ref, bf16[512,1536]{1,0:T(8,128)(2,1)} %feat_hbm.1, f32[24,768]{1,0:T(8,128)} %master_ref.1, f32[24]{0:T(128)} %rmom_ref.1, f32[768]{0:T(1024)} %cmom_ref.1, ...), custom_call_target="tpu_custom_call" | custom-call | tf_op jit(solution)/shard_map/adafactor_step/pallas_call | solution.py:611
  138.9 2.6 %results.1 = (f32[24,768]{1,0:T(8,128)}, f32[24]{0:T(128)}, f32[768]{0:T(1024)}, bf16[1536,768]{1,0:T(8,128)(2,1)}) custom-call(f32[24,768]{1,0:T(8,128)} %get-tuple-element.8.new_in, f32[24]{0:T(128)} %get-tuple-element.9.rstate_in, f32[768]{0:T(1024)} %get-tuple-element.10.cstate_in, bf16[1536,768]{1,0:T(8,128)(2,1)} %get-tuple-element.11.low_in), custom_call_target="tpu_custom_call" | custom-call | tf_op jit(solution)/shard_map/results/pallas_call | solution.py:664

commit v8 on v7

--- a/solution.py
+++ b/solution.py
@@ -143,7 +143,7 @@
         self.sent = []
 
     def index(self, x, z):
-        return x * NZ + lax.rem(z, 4) * 4 + lax.div(z, 4)
+        return lax.rem(z, 4) * 16 + lax.div(z, 4) * 4 + x
 
     def round(self, first, count, k, peers):
         for i, peer in enumerate(peers):
@@ -166,17 +166,17 @@
     def along(self, distances):
         return [(self.x * NZ + lax.rem(self.z + d, NZ), self.mp) for d in distances]
 
+    def across(self):
+        peers = [(lax.rem(self.x + d, NX) * NZ + self.z, self.mp) for d in (2, 1, 3)]
+        self.round(self.index(self.x, self.z), 1, 0, peers)
+
     def far(self):
-        self.round(self.index(self.x, self.z), 1, 0, self.along((8, 4, 12)))
+        self.arrived(0)
+        self.round(self.index(0, self.z), 4, 3, self.along((8, 4, 12)))
 
     def near(self):
-        self.arrived(0)
-        self.round(self.x * NZ + lax.rem(self.z, 4) * 4, 4, 3, self.along((2, 1, 15)))
-
-    def across(self):
         self.arrived(3)
-        peers = [(lax.rem(self.x + d, NX) * NZ + self.z, self.mp) for d in (2, 1, 3)]
-        self.round(self.x * NZ, NZ, 6, peers)
+        self.round(lax.rem(self.z, 4) * 16, 16, 6, self.along((2, 1, 15)))
 
     def finish(self):
         for copy in self.sent:
@@ -228,8 +228,8 @@
     new_ref, rstate_ref, cstate_ref, low_ref,
     wbuf, wtile, weight, nbuf, ntile, low, feat, grad_in, masked, masked_t, pre, dpre,
     partial, inverses, coded, xrecv, summed, near_coded, lrecv, far_coded, frecv, scale_src, scale_dst,
-    row_src, row_dst, vec, vec_in,
-    ag_send, ag_recv, ag2_send, ag2_recv, rs_send, rs_recv, row_send, row_recv, vec_send, vec_recv, wt_send, wt_recv, nt_send, nt_recv, load_sem,
+    row_src, row_dst, vec, vec_x, vec_z, vec_m,
+    ag_send, ag_recv, ag2_send, ag2_recv, rs_send, rs_recv, row_send, row_recv, vx_sem, vz_sem, vm_sem, wt_send, wt_recv, nt_send, nt_recv, load_sem,
 ):
     dp, mp = lax.axis_index("dp"), lax.axis_index("mp")
     x, z = lax.div(dp, NZ), lax.rem(dp, NZ)
@@ -243,7 +243,8 @@
     mp_peers = [(dp, lax.rem(mp + d, NMP)) for d in range(1, NMP)]
 
     barrier = pltpu.get_barrier_semaphore()
-    greeted = far_peers + near_peers + [at(0, NZ - 2)] + x_peers + mp_peers
+    z_peers = [at(0, d) for d in range(1, NZ)]
+    greeted = z_peers + x_peers + mp_peers
     for peer in greeted:
         pl.semaphore_signal(barrier, inc=1, device_id=peer, device_id_type=MESH)
 
@@ -269,7 +270,7 @@
     wtile[tiles.index(x, z)] = jnp.where(lane == 127, peak * (1.0 / 32767), moment_lanes)
 
     pl.semaphore_wait(barrier, len(greeted))
-    tiles.far()
+    tiles.across()
     gather = Gather(wbuf, ag_send, ag_recv, x, z, mp)
     gather.start()
 
@@ -291,10 +292,10 @@
     load_grad.wait()
     moment = to_rows(moment_lanes)
     for part, _ in enumerate(gather.events()):
-        if part == 2:
+        if part == 0:
+            tiles.far()
+        elif part == 2:
             tiles.near()
-        elif part == 3:
-            tiles.across()
     tiles.arrived(6)
 
     def weights(slot):
@@ -451,10 +452,6 @@
         far_copy(i).wait_recv()
         grad = grad + decode(frecv[i], unpack(scale_dst[6 + i]))
 
-    peak = scale_of(peak_of(grad))
-    nbuf[dp] = encode(grad, 32767.0 / peak)
-    regather = Gather(nbuf, ag2_send, ag2_recv, x, z, mp)
-    regather.start()
     squared = grad * grad
     row_lanes = squared[:, :128]
     for i in range(1, COLS // 128):
@@ -471,56 +468,69 @@
             device_id_type=MESH,
         )
 
-    def vec_copy(step, i):
-        return pltpu.make_async_remote_copy(
-            src_ref=vec.at[step],
-            dst_ref=vec_in.at[step, i],
-            send_sem=vec_send.at[step, i],
-            recv_sem=vec_recv.at[step, i],
-            device_id=(x_peers, far_peers, near_peers)[step][i],
-            device_id_type=MESH,
-        )
-
-    def vec_start(step):
-        for i in range(3):
-            vec_copy(step, i).start()
-
-    def vec_sum(step):
+    def vec_copies(step, landing, sems, peers):
+        return [
+            pltpu.make_async_remote_copy(
+                src_ref=vec.at[step],
+                dst_ref=landing.at[i],
+                send_sem=sems.at[0, i],
+                recv_sem=sems.at[1, i],
+                device_id=peer,
+                device_id_type=MESH,
+            )
+            for i, peer in enumerate(peers)
+        ]
+
+    rounds = [
+        vec_copies(0, vec_x, vx_sem, x_peers),
+        vec_copies(1, vec_z, vz_sem, z_peers),
+        vec_copies(2, vec_m, vm_sem, mp_peers),
+    ]
+
+    def begin(step):
+        for copy in rounds[step]:
+            copy.start()
+
+    def total_of(step, landing):
         sums = vec[step]
-        for i in range(3):
-            vec_copy(step, i).wait_recv()
-            sums = sums + vec_in[step, i]
+        for i, copy in enumerate(rounds[step]):
+            copy.wait_recv()
+            sums = sums + landing[i]
         return sums
 
+    column = jnp.sum(squared, axis=0, keepdims=True)
+    vec[0] = pack(column, jnp.sum(row_lanes, axis=0, keepdims=True), moment_lanes)
+    begin(0)
     for i in range(NMP - 1):
         row_copy(i).start()
-    column = jnp.sum(squared, axis=0, keepdims=True)
+    peak = scale_of(peak_of(grad))
+    nbuf[dp] = encode(grad, 32767.0 / peak)
+    regather = Gather(nbuf, ag2_send, ag2_recv, x, z, mp)
+    regather.start()
     events = regather.events()
     next(events)
 
+    vec[1] = total_of(0, vec_x)
+    begin(1)
     for i in range(NMP - 1):
         row_copy(i).wait_recv()
         row_lanes = row_lanes + row_dst[i]
-    vec[0] = pack(column, jnp.sum(row_lanes, axis=0, keepdims=True), moment_lanes)
-    vec_start(0)
     row_total = jnp.sum(row_lanes, axis=1, keepdims=True)
     retiles = Tiles(ntile, nt_send, nt_recv, x, z, mp)
     ntile[retiles.index(x, z)] = pack(peak * (1.0 / 32767), to_lanes(row_total))
+    retiles.across()
+    next(events)
+
     retiles.far()
     next(events)
-
-    vec[1] = vec_sum(0)
-    vec_start(1)
-    next(events)
-    vec[2] = vec_sum(1)
-    vec_start(2)
+    sums = total_of(1, vec_z)
+    vec[2] = sums
+    begin(2)
     retiles.near()
     next(events)
-    retiles.across()
-
-    sums = vec_sum(2)
+    norm = total_of(2, vec_m)[6:7]
     col_total = unpack(sums)
-    total = jnp.sum(sums[6:7], axis=1, keepdims=True)
+    total = jnp.sum(norm, axis=1, keepdims=True)
     moments = jnp.sum(sums[7:8], axis=1, keepdims=True)
 
     clip = 1.0 / jnp.maximum(1.0, jnp.sqrt(total / (D * FF)))
@@ -564,9 +574,9 @@
     retiles.finish()
     for i in range(NMP - 1):
         row_copy(i).wait_send()
-    for step in range(3):
-        for i in range(3):
-            vec_copy(step, i).wait_send()
+    for copies in rounds:
+        for copy in copies:
+            copy.wait_send()
     gather.finish()
     regather.finish()
     for d in (1, 2, 3):
@@ -641,7 +651,9 @@
             pltpu.VMEM((ROWS, 128), F32),
             pltpu.VMEM((NMP - 1, ROWS, 128), F32),
             pltpu.VMEM((3, 8, 128), F32),
-            pltpu.VMEM((3, 3, 8, 128), F32),
+            pltpu.VMEM((NX - 1, 8, 128), F32),
+            pltpu.VMEM((NZ - 1, 8, 128), F32),
+            pltpu.VMEM((NMP - 1, 8, 128), F32),
             pltpu.SemaphoreType.DMA((NX * NZ,)),
             pltpu.SemaphoreType.DMA((NX * NZ,)),
             pltpu.SemaphoreType.DMA((NX * NZ,)),
@@ -650,8 +662,9 @@
             pltpu.SemaphoreType.DMA((27,)),
             pltpu.SemaphoreType.DMA((NMP - 1,)),
             pltpu.SemaphoreType.DMA((NMP - 1,)),
-            pltpu.SemaphoreType.DMA((3, 3)),
-            pltpu.SemaphoreType.DMA((3, 3)),
+            pltpu.SemaphoreType.DMA((2, NX - 1)),
+            pltpu.SemaphoreType.DMA((2, NZ - 1)),
+            pltpu.SemaphoreType.DMA((2, NMP - 1)),
             pltpu.SemaphoreType.DMA((9,)),
             pltpu.SemaphoreType.DMA((9,)),
             pltpu.SemaphoreType.DMA((9,)),

time: 143 us -> 137 us (0.958)
  Pallas kernels: 140 us -> 133 us
    pallas_call x1, Pallas kernels: 137 us -> 131 us  [per_device(): pl.pallas_call(kernel, name='adafactor_step', out_shape=out_shape, in_spe...]
where the time goes in v8:
time: 137 us; the launch traced here: 135 us
  Pallas kernels  133 us (97%)
  between operations  1.93 us (1%)
    pallas_call x1, Pallas kernels, per_device(): pl.pallas_call(kernel, name='adafactor_step', out_shape=out_shape, in_spe...  131 us

profile of v8, /device:TPU:24, one launch (start us, length us, event | category | flops | bytes accessed | tf_op | source)
XLA Modules:
  0.0 135.3 jit_solution(126469610223833552)
XLA Ops:
  1.9 130.8 %adafactor_step.1 = (f32[24,768]{1,0:T(8,128)}, f32[24]{0:T(128)}, f32[768]{0:T(1024)}, bf16[1536,768]{1,0:T(8,128)(2,1)}) custom-call(s32[1]{0:T(128)S(6)} %copy.11.frame_ref, s32[1]{0:T(128)S(6)} %copy.12.chan_ref, bf16[512,1536]{1,0:T(8,128)(2,1)} %feat_hbm.1, f32[24,768]{1,0:T(8,128)} %master_ref.1, f32[24]{0:T(128)} %rmom_ref.1, f32[768]{0:T(1024)} %cmom_ref.1, ...), custom_call_target="tpu_custom_call" | custom-call | tf_op jit(solution)/shard_map/adafactor_step/pallas_call | solution.py:621
  132.7 2.6 %results.1 = (f32[24,768]{1,0:T(8,128)}, f32[24]{0:T(128)}, f32[768]{0:T(1024)}, bf16[1536,768]{1,0:T(8,128)(2,1)}) custom-call(f32[24,768]{1,0:T(8,128)} %get-tuple-element.8.new_in, f32[24]{0:T(128)} %get-tuple-element.9.rstate_in, f32[768]{0:T(1024)} %get-tuple-element.10.cstate_in, bf16[1536,768]{1,0:T(8,128)(2,1)} %get-tuple-element.11.low_in), custom_call_target="tpu_custom_call" | custom-call | tf_op jit(solution)/shard_map/results/pallas_call | solution.py:677

commit v9 on v8

--- a/solution.py
+++ b/solution.py
@@ -115,18 +115,11 @@
         self.relays(3, 5, 2, 11, 13, 10, 7, 9, 6)
         yield
 
-    def wait_block(self, d):
-        x = lax.rem(self.x + d, NX)
-
-        def step(i, _):
-            if d == 2:
-                owner = i
-            else:
-                owner = 2 * i + (0 if d == 1 else 1)
-            self.arrived(x * NZ + owner)
-            return 0
-
-        lax.fori_loop(0, NZ if d == 2 else NZ // 2, step, 0)
+    def wait_pair(self, d, slot):
+        if d in (1, 2):
+            self.arrived(slot)
+        if d in (3, 2):
+            self.arrived(slot + 1)
 
     def finish(self):
         def step(k, _):
@@ -224,12 +217,12 @@
 
 
 def kernel(
-    frame_ref, chan_ref, feat_hbm, master_ref, rmom_ref, cmom_ref, grad_hbm,
+    frame_ref, chan_ref, feat_hbm, master_hbm, rmom_hbm, cmom_hbm, grad_hbm,
     new_ref, rstate_ref, cstate_ref, low_ref,
-    wbuf, wtile, weight, nbuf, ntile, low, feat, grad_in, masked, masked_t, pre, dpre,
+    master_ref, rmom_ref, cmom_ref, wbuf, wtile, weight, nbuf, ntile, low, feat, grad_in, masked, masked_t, pre, dpre,
     partial, inverses, coded, xrecv, summed, near_coded, lrecv, far_coded, frecv, scale_src, scale_dst,
     row_src, row_dst, vec, vec_x, vec_z, vec_m,
-    ag_send, ag_recv, ag2_send, ag2_recv, rs_send, rs_recv, row_send, row_recv, vx_sem, vz_sem, vm_sem, wt_send, wt_recv, nt_send, nt_recv, load_sem,
+    ag_send, ag_recv, ag2_send, ag2_recv, rs_send, rs_recv, row_send, row_recv, vx_sem, vz_sem, vm_sem, wt_send, wt_recv, nt_send, nt_recv, load_sem, own_sem,
 ):
     dp, mp = lax.axis_index("dp"), lax.axis_index("mp")
     x, z = lax.div(dp, NZ), lax.rem(dp, NZ)
@@ -248,11 +241,19 @@
     for peer in greeted:
         pl.semaphore_signal(barrier, inc=1, device_id=peer, device_id_type=MESH)
 
+    own_loads = [
+        pltpu.make_async_copy(source, target, own_sem.at[i])
+        for i, (source, target) in enumerate(((master_hbm, master_ref), (rmom_hbm, rmom_ref), (cmom_hbm, cmom_ref)))
+    ]
+    for load in own_loads:
+        load.start()
     load_feat = pltpu.make_async_copy(feat_hbm, feat, load_sem.at[0])
     load_grad = pltpu.make_async_copy(grad_hbm, grad_in, load_sem.at[1])
     load_feat.start()
     load_grad.start()
 
+    for load in own_loads:
+        load.wait()
     master = master_ref[...]
     peak = jnp.max(scale_of(peak_of(master)), axis=1, keepdims=True)
     diag = lax.broadcasted_iota(jnp.int32, (ROWS, 128), 0) == lax.broadcasted_iota(jnp.int32, (ROWS, 128), 1)
@@ -302,9 +303,10 @@
         tile = wtile[tiles.index(lax.div(slot, NZ), lax.rem(slot, NZ))]
         return decode(wbuf[slot], tile[:, 127:128]), tile
 
-    def weight_block(block):
+    def weight_block(d, block):
         def step(i, _):
             slot = block * NZ + 2 * i
+            gather.wait_pair(d, slot)
             rows = pl.ds(pl.multiple_of(slot * ROWS, 2 * ROWS), 2 * ROWS)
             weight[rows, :] = stack(weights(slot)[0], weights(slot + 1)[0])
             return 0
@@ -313,9 +315,7 @@
 
     for d in (0, 1, 3, 2):
         block = lax.rem(x + d, NX)
-        if d:
-            gather.wait_block(d)
-        weight_block(block)
+        weight_block(d, block)
         depth = pl.ds(pl.multiple_of(block * BLOCK, BLOCK), BLOCK)
 
         def forward_tile(i, _, d=d, depth=depth):
@@ -559,11 +559,10 @@
 
     for d in (0, 1, 3, 2):
         block = lax.rem(x + d, NX)
-        if d:
-            regather.wait_block(d)
-
-        def update_pair(i, _, block=block):
+
+        def update_pair(i, _, d=d, block=block):
             slot = block * NZ + 2 * i
+            regather.wait_pair(d, slot)
             rows = pl.ds(pl.multiple_of(slot * ROWS, 2 * ROWS), 2 * ROWS)
             low[rows, :] = stack(updated(slot), updated(slot + 1))
             return 0
@@ -622,9 +621,12 @@
         kernel,
         name="adafactor_step",
         out_shape=out_shape,
-        in_specs=[smem, smem, anywhere, vmem, vmem, vmem, anywhere],
+        in_specs=[smem, smem, anywhere, anywhere, anywhere, anywhere, anywhere],
         out_specs=(vmem, vmem, vmem, anywhere),
         scratch_shapes=[
+            pltpu.VMEM((ROWS, COLS), F32),
+            pltpu.VMEM((ROWS,), F32),
+            pltpu.VMEM((COLS,), F32),
             pltpu.VMEM((NX * NZ, 2 * ROWS, HALF), I16),
             pltpu.VMEM((NX * NZ, 1, 128), F32),
             pltpu.VMEM((D, COLS), BF16),
@@ -670,6 +672,7 @@
             pltpu.SemaphoreType.DMA((9,)),
             pltpu.SemaphoreType.DMA((9,)),
             pltpu.SemaphoreType.DMA((2 + NX,)),
+            pltpu.SemaphoreType.DMA((3,)),
         ],
         compiler_params=pltpu.CompilerParams(collective_id=0, has_side_effects=True, vmem_limit_bytes=56 * 2**20),
     )(frame_start, chan_start, features, master_weight, row_moment, col_moment, out_grad)

time: 137 us -> 136 us (level)
  no operation moved by 1% of the time
where the time goes in v9:
time: 136 us; the launch traced here: 135 us
  Pallas kernels  133 us (98%)
  between operations  1.93 us (1%)
    pallas_call x1, Pallas kernels, per_device(): pl.pallas_call(kernel, name='adafactor_step', out_shape=out_shape, in_spe...  131 us

profile of v9, /device:TPU:24, one launch (start us, length us, event | category | flops | bytes accessed | tf_op | source)
XLA Modules:
  0.0 135.4 jit_solution(10409096571813671607)
XLA Ops:
  1.9 130.8 %adafactor_step.1 = (f32[24,768]{1,0:T(8,128)}, f32[24]{0:T(128)}, f32[768]{0:T(1024)}, bf16[1536,768]{1,0:T(8,128)(2,1)}) custom-call(s32[1]{0:T(128)S(6)} %copy.11.frame_ref, s32[1]{0:T(128)S(6)} %copy.12.chan_ref, bf16[512,1536]{1,0:T(8,128)(2,1)} %feat_hbm.1, f32[24,768]{1,0:T(8,128)} %master_hbm.1, f32[24]{0:T(128)} %rmom_hbm.1, f32[768]{0:T(1024)} %cmom_hbm.1, ...), custom_call_target="tpu_custom_call" | custom-call | tf_op jit(solution)/shard_map/adafactor_step/pallas_call | solution.py:620
  132.8 2.6 %results.1 = (f32[24,768]{1,0:T(8,128)}, f32[24]{0:T(128)}, f32[768]{0:T(1024)}, bf16[1536,768]{1,0:T(8,128)(2,1)}) custom-call(f32[24,768]{1,0:T(8,128)} %get-tuple-element.8.new_in, f32[24]{0:T(128)} %get-tuple-element.9.rstate_in, f32[768]{0:T(1024)} %get-tuple-element.10.cstate_in, bf16[1536,768]{1,0:T(8,128)(2,1)} %get-tuple-element.11.low_in), custom_call_target="tpu_custom_call" | custom-call | tf_op jit(solution)/shard_map/results/pallas_call | solution.py:680

commit v10 on v9

--- a/solution.py
+++ b/solution.py
@@ -218,7 +218,8 @@
 
 def kernel(
     frame_ref, chan_ref, feat_hbm, master_hbm, rmom_hbm, cmom_hbm, grad_hbm,
-    new_ref, rstate_ref, cstate_ref, low_ref,
+    new_hbm, rstate_hbm, cstate_hbm, low_ref,
+    new_ref, rstate_ref, cstate_ref,
     master_ref, rmom_ref, cmom_ref, wbuf, wtile, weight, nbuf, ntile, low, feat, grad_in, masked, masked_t, pre, dpre,
     partial, inverses, coded, xrecv, summed, near_coded, lrecv, far_coded, frecv, scale_src, scale_dst,
     row_src, row_dst, vec, vec_x, vec_z, vec_m,
@@ -545,6 +546,12 @@
     new_ref[...] = master_ref[...] - grad * (lax.rsqrt(row_state / row_mean) * col_factor)
     rstate_ref[...] = to_lanes(row_state)[:, :ROWS].reshape(ROWS)
     cstate_ref[...] = col_state.reshape(COLS)
+    own_stores = [
+        pltpu.make_async_copy(source, target, own_sem.at[3 + i])
+        for i, (source, target) in enumerate(((new_ref, new_hbm), (rstate_ref, rstate_hbm), (cstate_ref, cstate_hbm)))
+    ]
+    for store in own_stores:
+        store.start()
     retiles.arrived(6)
 
     def updated(slot):
@@ -589,6 +596,8 @@
         far_copy(i).wait_send()
     for d in range(NX):
         leave(d).wait()
+    for store in own_stores:
+        store.wait()
 
 
 def copy_kernel(new_in, rstate_in, cstate_in, low_in, new_out, rstate_out, cstate_out, low_out, new, rstate, cstate, low, sem):
@@ -608,7 +617,6 @@
 
 
 def per_device(features, frame_start, chan_start, master_weight, row_moment, col_moment, out_grad):
-    vmem = pl.BlockSpec(memory_space=pltpu.VMEM)
     smem = pl.BlockSpec(memory_space=pltpu.SMEM)
     out_shape = (
         jax.ShapeDtypeStruct((ROWS, COLS), F32),
@@ -622,8 +630,11 @@
         name="adafactor_step",
         out_shape=out_shape,
         in_specs=[smem, smem, anywhere, anywhere, anywhere, anywhere, anywhere],
-        out_specs=(vmem, vmem, vmem, anywhere),
+        out_specs=(anywhere,) * 4,
         scratch_shapes=[
+            pltpu.VMEM((ROWS, COLS), F32),
+            pltpu.VMEM((ROWS,), F32),
+            pltpu.VMEM((COLS,), F32),
             pltpu.VMEM((ROWS, COLS), F32),
             pltpu.VMEM((ROWS,), F32),
             pltpu.VMEM((COLS,), F32),
@@ -672,7 +683,7 @@
             pltpu.SemaphoreType.DMA((9,)),
             pltpu.SemaphoreType.DMA((9,)),
             pltpu.SemaphoreType.DMA((2 + NX,)),
-            pltpu.SemaphoreType.DMA((3,)),
+            pltpu.SemaphoreType.DMA((6,)),
         ],
         compiler_params=pltpu.CompilerParams(collective_id=0, has_side_effects=True, vmem_limit_bytes=56 * 2**20),
     )(frame_start, chan_start, features, master_weight, row_moment, col_moment, out_grad)

time: 136 us -> 135 us (level)
  no operation moved by 1% of the time
where the time goes in v10:
time: 135 us
  Pallas kernels  133 us (99%)
  between operations  1.93 us (1%)
    pallas_call x1, Pallas kernels, per_device(): pl.pallas_call(kernel, name='adafactor_step', out_shape=out_shape, in_spe...  130 us

profile of v10, /device:TPU:24, one launch (start us, length us, event | category | flops | bytes accessed | tf_op | source)
XLA Modules:
  0.0 135.0 jit_solution(6555318373577651591)
XLA Ops:
  1.9 130.5 %adafactor_step.1 = (f32[24,768]{1,0:T(8,128)}, f32[24]{0:T(128)}, f32[768]{0:T(1024)}, bf16[1536,768]{1,0:T(8,128)(2,1)}) custom-call(s32[1]{0:T(128)S(6)} %copy.11.frame_ref, s32[1]{0:T(128)S(6)} %copy.12.chan_ref, bf16[512,1536]{1,0:T(8,128)(2,1)} %feat_hbm.1, f32[24,768]{1,0:T(8,128)} %master_hbm.1, f32[24]{0:T(128)} %rmom_hbm.1, f32[768]{0:T(1024)} %cmom_hbm.1, ...), custom_call_target="tpu_custom_call" | custom-call | tf_op jit(solution)/shard_map/adafactor_step/pallas_call | solution.py:628
  132.4 2.6 %results.1 = (f32[24,768]{1,0:T(8,128)}, f32[24]{0:T(128)}, f32[768]{0:T(1024)}, bf16[1536,768]{1,0:T(8,128)(2,1)}) custom-call(f32[24,768]{1,0:T(8,128)} %get-tuple-element.8.new_in, f32[24]{0:T(128)} %get-tuple-element.9.rstate_in, f32[768]{0:T(1024)} %get-tuple-element.10.cstate_in, bf16[1536,768]{1,0:T(8,128)(2,1)} %get-tuple-element.11.low_in), custom_call_target="tpu_custom_call" | custom-call | tf_op jit(solution)/shard_map/results/pallas_call | solution.py:691
